TPU v7x, 512 devices: a whole 4x8x8 slice. The times are simulated.
512 devices in a mesh: ap: 128 (over z_hi, y, x), sec: 4 (over z_lo, core).
Axes of the slice: x: 4, y: 8, z: 8 (z_hi: 4, z_lo: 2; z = z_hi * 2 + z_lo), core: 2. Of those that a mesh axis runs over, the one named last changes fastest.
Arguments:
- polar: bfloat16 [128, 2, 2048, 1024], P('ap', None, 'sec'), may hold values from -128 to 128
- autofocus: float32 [2, 2, 128, 1024], P(None, None, 'ap'), may hold values from -3.140625 to 3.140625
- offsets: int32 [2, 2, 128, 2048], P(None, None, 'ap', 'sec'), may hold values from 0 to 504, as said below
- weights: float32 [2, 2, 128, 8, 2048], P(None, None, 'ap', None, 'sec'), may hold values from -2.4 to 2.4
Outputs:
- merged: bfloat16 [128, 2, 2048, 1024], P('ap', None, 'sec')
Inputs may be any that keep to these rules, and one draw needn't show every extreme that they name: `offsets`: for target s at section k, with b the bit k of s, every offset lies from b * (248) to b * 248 + 512 // 2 + 8 - 8.
All inputs are finite; a program needn't handle non-finite values.
Results may differ from a plain program's by a relative error of at most 0.007.
Values may be sent and summed in bfloat16 or wider, within the bound.
No kernel may reach another device: no remote copies, remote signals or barrier semaphores. Data moves between devices by JAX's collectives and lax.ppermute only.
A program may use at most 64 MiB of HBM per device.

v0:
```python
import jax
import jax.numpy as jnp
from jax import lax
from jax.sharding import PartitionSpec as P

SECTIONS = 2


def partner(value, axis, distance):
    return lax.ppermute(value, axis, [(i, i ^ 1 << distance) for i in range(lax.axis_size(axis))])


def interpolate(block_rows, offset_rows, tap_weights, phase_turn, band_start):
    source_index = (
        lax.broadcasted_iota(jnp.int32, (offset_rows.shape[0], block_rows.shape[1]), 1) + band_start
    )
    interp_table = jnp.zeros(source_index.shape, jnp.float32)
    for tap_index in range(tap_weights.shape[0]):
        matches = source_index == (offset_rows + tap_index)[:, None]
        interp_table = interp_table + jnp.where(matches, tap_weights[tap_index][:, None], 0.0)
    interp_table = interp_table.astype(jnp.bfloat16)
    interpolated = jnp.einsum(
        "js,csr->cjr", interp_table, block_rows, preferred_element_type=jnp.float32
    )
    cosine = jnp.cos(phase_turn)
    sine_part = jnp.sin(phase_turn)
    real_part = cosine * interpolated[0] - sine_part * interpolated[1]
    imag_part = sine_part * interpolated[0] + cosine * interpolated[1]
    return (real_part, imag_part)


def shards(polar, autofocus, offsets, weights):
    picture = polar[0]
    own_energy = jnp.sum(jnp.square(picture.astype(jnp.float32)))
    energy_sum = lax.psum(own_energy, "sec")
    cell_count = picture.shape[1] * lax.axis_size("sec") * picture.shape[2]
    energy_gain = lax.rsqrt(energy_sum / cell_count + 1e-06)
    picture = (picture.astype(jnp.float32) * energy_gain).astype(jnp.bfloat16)
    aperture = lax.axis_index("ap")
    for merge_step in range(SECTIONS):
        half_index = aperture // 2**merge_step % 2
        band_start = 0
        own_block = picture
        peer_block = partner(picture, "ap", merge_step)
        step_offsets = offsets[merge_step, :, 0]
        step_weights = weights[merge_step, :, 0]
        step_phase = autofocus[merge_step, :, 0]
        own_real, own_imag = interpolate(
            own_block,
            lax.dynamic_index_in_dim(step_offsets, half_index, 0, keepdims=False),
            lax.dynamic_index_in_dim(step_weights, half_index, 0, keepdims=False),
            lax.dynamic_index_in_dim(step_phase, half_index, 0, keepdims=False),
            band_start,
        )
        peer_real, peer_imag = interpolate(
            peer_block,
            lax.dynamic_index_in_dim(step_offsets, 1 - half_index, 0, keepdims=False),
            lax.dynamic_index_in_dim(step_weights, 1 - half_index, 0, keepdims=False),
            lax.dynamic_index_in_dim(step_phase, 1 - half_index, 0, keepdims=False),
            band_start,
        )
        picture = jnp.stack([own_real + peer_real, own_imag + peer_imag]).astype(jnp.bfloat16)
    return picture[None]


def solution(mesh):
    placed = (
        P("ap", None, "sec", None),
        P(None, None, "ap", None),
        P(None, None, "ap", "sec"),
        P(None, None, "ap", None, "sec"),
    )
    return jax.shard_map(
        shards, mesh=mesh, in_specs=placed, out_specs=P("ap", None, "sec", None), check_vma=False
    )
```

profile of v0, /device:TPU:1, one launch (start us, length us, event | category | flops | bytes accessed | tf_op | source)
XLA Modules:
  0.0 131.6 jit_solution(8867938633762491653)
XLA Ops:
  0.0 2.9 %copy.5 = bf16[1,2,512,1024]{2,3,1,0:T(8,128)(2,1)S(1)} copy(bf16[1,2,512,1024]{3,2,1,0:T(8,128)(2,1)} %param.4) | data formatting | bytes 4194304 | tf_op args[0]
  2.9 1.7 %fusion = f32[]{:T(128)} fusion(bf16[1,2,512,1024]{2,3,1,0:T(8,128)(2,1)S(1)} %copy.5), kind=kLoop, calls=%fused_computation.2 | loop fusion | flops 3145727 | bytes 2097156 | tf_op jit(solution)/shard_map/reduce_sum | solution.py:34
  4.5 12.5 %psum.7 = f32[]{:T(128)} all-reduce(f32[]{:T(128)} %fusion), channel_id=1, replica_groups=mesh['ap'=128,'sec'=4] {'sec'}, use_global_device_ids=true, to_apply=%region_1.0 | all-reduce | flops 1 | bytes 8 | tf_op jit(solution)/shard_map/psum | solution.py:35
  17.7 0.0 copy-start.2
  17.7 0.0 copy-start.1
  17.8 0.0 copy-start
  17.8 1.7 %fusion.2 = bf16[2,512,1024]{1,2,0:T(8,128)(2,1)} fusion(bf16[1,2,512,1024]{2,3,1,0:T(8,128)(2,1)S(1)} %copy.5, f32[]{:T(128)S(6)} %rsqrt.3), kind=kLoop, calls=%fused_computation.8 | loop fusion | flops 3145728 | bytes 4194308 | tf_op jit(solution)/shard_map/convert_element_type | solution.py:38
  19.5 1.9 %collective-permute-start = (bf16[2,512,1024]{1,2,0:T(8,128)(2,1)}, bf16[2,512,1024]{1,2,0:T(8,128)(2,1)S(1)}, u32[]{:S(2)}, u32[]{:S(2)}) collective-permute-start(bf16[2,512,1024]{1,2,0:T(8,128)(2,1)} %fusion.2), channel_id=1, source_target_pairs={{0,4},{4,0},{8,12},{12,8},{16,20},{20,16},{24,28},{28,24},{32,36},... | collective-permute-start | bytes 6291464 | tf_op jit(solution)/shard_map/ppermute | solution.py:10
  21.5 0.0 copy-done.2
  21.5 0.0 copy-done.1
  21.5 0.5 fusion.81
  22.0 0.0 copy-done
  22.0 0.1 constant_dynamic-slice_fusion.6
  22.2 4.2 %convolution_bitcast_fusion.3 = f32[2,512,1024]{1,2,0:T(8,128)S(1)} fusion(bf16[2,512,1024]{1,2,0:T(8,128)(2,1)} %fusion.2, f32[512]{0:T(512)S(1)} %bitcast.113, s32[512]{0:T(512)S(1)} %get-tuple-element.74, f32[512]{0:T(512)S(1)} %bitcast.119, s32[512]{0:T(512)S(1)} %get-tuple-element.75, f32[512]{0:T(512)S(1)} %bitcast.118, s32[512]{0:T(512)S(1)} %get-tuple-element.76, ...), kind=kOutput, calls=%fused_computation.7 | convolution fusion | flops 1080033280 | bytes 6324224 | tf_op jit(solution)/shard_map/js,csr->cjr/dot_general | solution.py:22
  26.4 41.6 %collective-permute-done = bf16[2,512,1024]{1,2,0:T(8,128)(2,1)S(1)} collective-permute-done((bf16[2,512,1024]{1,2,0:T(8,128)(2,1)}, bf16[2,512,1024]{1,2,0:T(8,128)(2,1)S(1)}, u32[]{:S(2)}, u32[]{:S(2)}) %collective-permute-start) | collective-permute-done | bytes 2097184 | tf_op jit(solution)/shard_map/ppermute | solution.py:10
  68.0 4.7 %convolution_bitcast_fusion.2 = f32[2,512,1024]{1,2,0:T(8,128)S(1)} fusion(bf16[2,512,1024]{1,2,0:T(8,128)(2,1)S(1)} %collective-permute-done, f32[512]{0:T(512)S(1)} %bitcast.105, s32[512]{0:T(512)S(1)} %get-tuple-element.81, f32[512]{0:T(512)S(1)} %bitcast.112, s32[512]{0:T(512)S(1)} %get-tuple-element.82, f32[512]{0:T(512)S(1)} %bitcast.111, ...), kind=kOutput, calls=%fused_computation.6 | convolution fusion | flops 1080033280 | bytes 6324224 | tf_op jit(solution)/shard_map/js,csr->cjr/dot_general | solution.py:22
  72.7 1.3 add_convert_fusion.3
  74.0 0.2 pad_maximum_fusion
  74.2 2.1 %collective-permute-start.1 = (bf16[2,512,1024]{1,2,0:T(8,128)(2,1)S(1)}, bf16[2,512,1024]{1,2,0:T(8,128)(2,1)S(1)}, u32[]{:S(2)}, u32[]{:S(2)}) collective-permute-start(bf16[2,512,1024]{1,2,0:T(8,128)(2,1)S(1)} %pad_maximum_fusion), channel_id=1, source_target_pairs={{0,8},{4,12},{8,0},{12,4},{16,24},{20,28},{24,16},{28,20},{32,40},... | collective-permute-start | bytes 6291464 | tf_op jit(solution)/shard_map/ppermute | solution.py:10
  76.3 2.7 %convolution_bitcast_fusion.1 = f32[2,512,1024]{1,2,0:T(8,128)S(1)} fusion(f32[512]{0:T(512)S(1)} %bitcast.104, s32[512]{0:T(512)S(1)} %get-tuple-element.60, f32[512]{0:T(512)S(1)} %bitcast.98, s32[512]{0:T(512)S(1)} %get-tuple-element.61, f32[512]{0:T(512)S(1)} %bitcast.99, s32[512]{0:T(512)S(1)} %get-tuple-element.62, f32[512]{0:T(512)S(1)} %bitcast.100, ...), kind=kOutput, calls=%fused_computation.5 | convolution fusion | flops 1081081856 | bytes 6324224 | tf_op jit(solution)/shard_map/js,csr->cjr/dot_general | solution.py:22
  79.1 44.0 %collective-permute-done.1 = bf16[2,512,1024]{1,2,0:T(8,128)(2,1)S(1)} collective-permute-done((bf16[2,512,1024]{1,2,0:T(8,128)(2,1)S(1)}, bf16[2,512,1024]{1,2,0:T(8,128)(2,1)S(1)}, u32[]{:S(2)}, u32[]{:S(2)}) %collective-permute-start.1) | collective-permute-done | bytes 2097184 | tf_op jit(solution)/shard_map/ppermute | solution.py:10
  123.1 4.7 %convolution_bitcast_fusion = f32[2,512,1024]{1,2,0:T(8,128)S(1)} fusion(bf16[2,512,1024]{1,2,0:T(8,128)(2,1)S(1)} %collective-permute-done.1, f32[512]{0:T(512)S(1)} %bitcast.96, s32[512]{0:T(512)S(1)} %get-tuple-element.67, f32[512]{0:T(512)S(1)} %bitcast.89, s32[512]{0:T(512)S(1)} %get-tuple-element.68, f32[512]{0:T(512)S(1)} %bitcast.90, ...), kind=kOutput, calls=%fused_computation.4 | convolution fusion | flops 1080033280 | bytes 6324224 | tf_op jit(solution)/shard_map/js,csr->cjr/dot_general | solution.py:22
  127.8 1.3 fusion.3
  129.1 0.2 pad_maximum_fusion.1
  129.3 2.4 %copy.6 = bf16[1,2,512,1024]{3,2,1,0:T(8,128)(2,1)} copy(bf16[1,2,512,1024]{2,3,1,0:T(8,128)(2,1)S(1)} %pad_maximum_fusion.1) | data formatting | bytes 4194304 | tf_op jit(solution)/shard_map/stack | solution.py:62
  (8 shorter events, 0.1 us)
Async XLA Ops:
  17.7 3.7 %copy-start.2 = (s32[2,2,1,512]{3,2,1,0:T(1,128)S(1)}, s32[2,2,1,512]{3,2,1,0:T(1,128)}, u32[]{:S(2)}) copy-start(s32[2,2,1,512]{3,2,1,0:T(1,128)} %param.6) | copy-start | bytes 24580
  17.7 3.8 %copy-start.1 = (f32[2,2,1,1024]{3,2,1,0:T(1,128)S(1)}, f32[2,2,1,1024]{3,2,1,0:T(1,128)}, u32[]{:S(2)}) copy-start(f32[2,2,1,1024]{3,2,1,0:T(1,128)} %param.5) | copy-start | bytes 49156
  17.8 4.3 %copy-start = (f32[2,2,1,8,512]{4,3,2,1,0:T(8,128)S(1)}, f32[2,2,1,8,512]{4,3,2,1,0:T(8,128)}, u32[]{:S(2)}) copy-start(f32[2,2,1,8,512]{4,3,2,1,0:T(8,128)} %param.7) | copy-start | bytes 196612
  19.5 48.5 %collective-permute-start = (bf16[2,512,1024]{1,2,0:T(8,128)(2,1)}, bf16[2,512,1024]{1,2,0:T(8,128)(2,1)S(1)}, u32[]{:S(2)}, u32[]{:S(2)}) collective-permute-start(bf16[2,512,1024]{1,2,0:T(8,128)(2,1)} %fusion.2), channel_id=1, source_target_pairs={{0,4},{4,0},{8,12},{12,8},{16,20},{20,16},{24,28},{28,24},{32,36},... | collective-permute-start | bytes 6291464 | tf_op jit(solution)/shard_map/ppermute | solution.py:10
  74.2 48.9 %collective-permute-start.1 = (bf16[2,512,1024]{1,2,0:T(8,128)(2,1)S(1)}, bf16[2,512,1024]{1,2,0:T(8,128)(2,1)S(1)}, u32[]{:S(2)}, u32[]{:S(2)}) collective-permute-start(bf16[2,512,1024]{1,2,0:T(8,128)(2,1)S(1)} %pad_maximum_fusion), channel_id=1, source_target_pairs={{0,8},{4,12},{8,0},{12,4},{16,24},{20,28},{24,16},{28,20},{32,40},... | collective-permute-start | bytes 6291464 | tf_op jit(solution)/shard_map/ppermute | solution.py:10
where the time goes:
time: 132 us
  waiting for transfers between devices  85.6 us (65%)
  matrix products  16.3 us (12%)
  blocking collectives  12.5 us (9%)
  other arithmetic  6.4 us (5%)
  local copies, waits for them, and re-layouts  5.9 us (4%)
  starting transfers between devices  4.01 us (3%)
    ppermute x2, waiting for transfers between devices, partner(): lax.ppermute(value, axis, [(i, i ^ 1 << distance) for i in range(lax.axis...  85.6 us
    dot_general x4, matrix products, interpolate(): jnp.einsum('js,csr->cjr', interp_table, block_rows, preferred_element_typ...  16.3 us
    psum x1, blocking collectives, shards(): energy_sum = lax.psum(own_energy, 'sec')  12.5 us
    ppermute x2, starting transfers between devices, partner(): lax.ppermute(value, axis, [(i, i ^ 1 << distance) for i in range(lax.axis...  4.01 us
    unnamed x7, local copies, waits for them, and re-layouts  2.87 us
  transfers between devices with their start and end apart: 2, of which 2 were waited for; matrix products, arithmetic and copies ran while one was open for 6% of the time, Pallas kernels for 0%

commit v1 on v0

v1 whole, which is shorter than its diff:
```python
import functools

import jax
import jax.numpy as jnp
from jax import lax
from jax.experimental import pallas as pl
from jax.experimental.pallas import tpu as pltpu
from jax.sharding import Mesh
from jax.sharding import PartitionSpec as P

GROUP = 4
TILE = 8
STEP = 31
SPAN = 33
BAND = SPAN * TILE
BULK = 256
TAPS = 8
LANES = 128
BLOCK = 256
OUT_ROWS = 256
FAR_PARTS = (768, 256)
NEAR_PARTS = (512, 256, 256)
DATA_TILES = 8
PIECES = 4
TERMS = 3


def partner(value, flip):
    return lax.ppermute(value, "x", [(i, i ^ flip) for i in range(GROUP)])


def terms_of(value):
    terms = []
    for _ in range(TERMS):
        terms.append(value.astype(jnp.bfloat16).astype(jnp.float32))
        value = value - terms[-1]
    return terms


def place_bits():
    place = lax.axis_index("x")
    return place % 2, place // 2


def encode(tail, bit, weights, offsets, phases):
    beams = weights.shape[-1]
    own = bit == 0
    starts, angles = [], []
    for child in range(2):
        lanes = slice(child * beams, (child + 1) * beams)
        taps = jnp.where(own, weights[child, 0], weights[1 - child, 0])
        tail[0, :, lanes] = taps.astype(jnp.bfloat16)
        start = jnp.where(own, offsets[child], offsets[1 - child]) - bit * (STEP * TILE)
        starts.append(start.astype(jnp.float32))
        angles += terms_of(jnp.where(own, phases[child], phases[1 - child]))
    rows = [jnp.concatenate(starts, axis=1)] + angles
    rows.append(jnp.zeros((TILE - len(rows), 2 * beams), jnp.float32))
    tail[1] = jnp.concatenate(rows).astype(jnp.bfloat16)


def decode(data):
    if data.shape[0] == 2:
        return data[0].astype(jnp.float32), data[1].astype(jnp.float32)
    at, each = 2 * SPAN + 1, DATA_TILES // 2
    return [
        jnp.concatenate([data[at + i * each + k].astype(jnp.float32) for k in range(each)], axis=1) for i in range(2)
    ]


def section_specs(section, *arrays):
    def spec(shape):
        return pl.BlockSpec((1, *shape[1:]), lambda i: (section,) + (0,) * (len(shape) - 1))

    return [spec(array.shape) for array in arrays]


def prepare_kernel(*refs):
    low, high = place_bits()
    sections, rows = (refs[0:3], refs[3:6]), refs[6]
    far, *near, energy, near_data, last_data, image, sems = refs[7:]
    piece = image.shape[1] // PIECES
    loads = []
    for k in range(PIECES):
        some = pl.ds(k * piece, piece)
        loads.append(pltpu.make_async_copy(rows.at[:, some], image.at[:, some], sems.at[k]))
        loads[-1].start()
    for data, bit, section in zip((near_data, last_data), (low, high), sections):
        encode(data, bit, *(array.at[0] for array in section))
    width, each = far.shape[-1], DATA_TILES // 2
    for i in range(2):
        for k in range(each):
            far[2 * SPAN + 1 + i * each + k] = near_data[i, :, k * width : (k + 1) * width]

    def add(i, total):
        block = image[:, pl.ds(i * 4, 4)].astype(jnp.float32)
        return total + jnp.sum(block * block, axis=(0, 1))

    total = jnp.zeros(image.shape[2:], jnp.float32)
    for k in range(PIECES):
        loads[k].wait()
        total = lax.fori_loop(k * piece // 4, (k + 1) * piece // 4, add, total)
    energy[...] = jnp.broadcast_to(jnp.sum(total, keepdims=True), energy.shape)
    for half in range(2):
        place = slice(half * SPAN, (half + 1) * SPAN)
        far[place] = image[half, pl.ds(low * STEP, SPAN), :, FAR_PARTS[0] :]
        at = 0
        for part in near:
            width = part.shape[-1]
            part[place] = image[half, pl.ds((1 - low) * STEP, SPAN), :, at : at + width]
            at += width


def prepare(rows, section):
    bins = rows.shape[-1]
    sizes = [(2 * SPAN + 1 + DATA_TILES, FAR_PARTS[1])] + [(2 * SPAN + (i == 0), w) for i, w in enumerate(NEAR_PARTS)]
    shapes = [jax.ShapeDtypeStruct((tiles, TILE, w), rows.dtype) for tiles, w in sizes]
    shapes.append(jax.ShapeDtypeStruct((1, LANES), jnp.float32))
    shapes += [jax.ShapeDtypeStruct((2, TILE, bins), rows.dtype)] * 2
    return pl.pallas_call(
        prepare_kernel,
        grid=(1,),
        out_shape=shapes,
        in_specs=[*section_specs(0, *section), *section_specs(1, *section), pl.BlockSpec(memory_space=pl.ANY)],
        out_specs=[pl.BlockSpec(memory_space=pltpu.VMEM)] * len(shapes),
        scratch_shapes=[pltpu.VMEM(rows.shape, rows.dtype), pltpu.SemaphoreType.DMA((PIECES,))],
        compiler_params=pltpu.CompilerParams(vmem_limit_bytes=52 * 2**20),
        cost_estimate=pl.CostEstimate(flops=4 * SPAN * TILE * bins, bytes_accessed=4_000_000, transcendentals=0),
        name="prepare",
    )(*section, *section, rows)


def seal_kernel(far, near, energy, far_result, near_result, tail, sems):
    row = lax.broadcasted_iota(jnp.int32, (TILE, LANES), 0)
    value = jnp.zeros((TILE, LANES), jnp.float32)
    for i, term in enumerate(terms_of(energy[...])):
        value = jnp.where(row == i, term, value)
    tail[0] = value.astype(jnp.bfloat16)
    copies = [
        pltpu.make_async_copy(tail, result.at[pl.ds(2 * SPAN, 1), :, 0:LANES], sems.at[i])
        for i, result in enumerate((far_result, near_result))
    ]
    for copy in copies:
        copy.start()
    for copy in copies:
        copy.wait()


def seal(far, near, energy):
    anywhere = pl.BlockSpec(memory_space=pl.ANY)
    return pl.pallas_call(
        seal_kernel,
        out_shape=[jax.ShapeDtypeStruct(part.shape, part.dtype) for part in (far, near)],
        in_specs=[anywhere, anywhere, pl.BlockSpec(memory_space=pltpu.VMEM)],
        out_specs=[anywhere, anywhere],
        scratch_shapes=[pltpu.VMEM((1, TILE, LANES), far.dtype), pltpu.SemaphoreType.DMA((2,))],
        input_output_aliases={0: 0, 1: 1},
        compiler_params=pltpu.CompilerParams(vmem_limit_bytes=4 * 2**20),
        cost_estimate=pl.CostEstimate(flops=10_000, bytes_accessed=20_000, transcendentals=0),
        name="seal",
    )(far, near, energy)


def build_table(target, columns, first_row, row_tiles, group):
    rows = group * TILE
    lane = lax.broadcasted_iota(jnp.int32, (rows, LANES), 1)

    def step(i, carry):
        block = columns[pl.ds(pl.multiple_of(first_row + i * rows, TILE), rows), :]
        place = pl.ds(pl.multiple_of(i * rows, TILE), rows)

        def spread(column):
            return jnp.broadcast_to(block[:, column : column + 1], (rows, LANES))

        rest = jnp.zeros((rows, LANES), jnp.float32)
        for child in range(2):
            start = spread(2 * TAPS + child).astype(jnp.int32)
            taps = [spread(child * TAPS + t) for t in range(TAPS)]

            def entries(source, part):
                hit = source - start
                for t in range(TAPS):
                    part = jnp.where(hit == t, taps[t], part)
                return part

            for part in range(BULK // LANES):
                at = child * BULK + part * LANES
                target[place, at : at + LANES] = entries(lane + part * LANES, jnp.zeros((rows, LANES), jnp.float32))
            inside = (lane >= child * TILE) & (lane < (child + 1) * TILE)
            rest = entries(jnp.where(inside, lane + (BULK - child * TILE), -TAPS), rest)
        target[place, 2 * BULK : 2 * BAND] = rest[:, : 2 * TILE]
        return carry

    lax.fori_loop(0, row_tiles // group, step, 0)


def table_kernel(data, table, turn, columns):
    beams = columns.shape[0]
    taps, rest = decode(data)
    starts = jnp.concatenate([rest[:1, :beams], rest[:1, beams:], jnp.zeros((TILE - 2, beams), jnp.float32)])
    fill = jnp.zeros((LANES - 2 * TAPS - TILE, beams), jnp.float32)
    columns[...] = jnp.transpose(jnp.concatenate([taps[:, :beams], taps[:, beams:], starts, fill]))
    for child in range(2):
        at = 1 + child * TERMS
        phase = rest[at : at + 1] + rest[at + 1 : at + 2] + rest[at + 2 : at + 3]
        turn[2 * child : 2 * child + 1, :] = jnp.cos(phase)
        turn[2 * child + 1 : 2 * child + 2, :] = jnp.sin(phase)
    first_row = place_bits()[1] * (STEP * TILE) if table.shape[0] == BAND else 0
    row_tiles = table.shape[0] // TILE
    build_table(table, columns, first_row, row_tiles, 3 if row_tiles % 3 == 0 else 4)


def make_table(rows, data, beams):
    whole = pl.BlockSpec(memory_space=pltpu.VMEM)
    table, turn = pl.pallas_call(
        table_kernel,
        out_shape=[jax.ShapeDtypeStruct(s, jnp.float32) for s in ((rows, 2 * BAND), (4, 2 * beams))],
        in_specs=[whole],
        out_specs=[whole] * 2,
        scratch_shapes=[pltpu.VMEM((beams, LANES), jnp.float32)],
        compiler_params=pltpu.CompilerParams(vmem_limit_bytes=8 * 2**20),
        cost_estimate=pl.CostEstimate(flops=rows * 12_000, bytes_accessed=rows * 4096, transcendentals=8192),
        name="table",
    )(data)
    return table.astype(jnp.bfloat16), turn


def turned(real, imag, cosine, sine):
    return cosine * real - sine * imag, sine * real + cosine * imag


def joined(left, right):
    both = []
    for a, b in zip(left, right):
        both.append(jnp.concatenate([a[:BULK], b[:BULK], a[BULK:], b[BULK:]]).astype(jnp.bfloat16))
    return jnp.concatenate(both, axis=1)


def first_merges(images, tables, turns, gains):
    width = images[1].shape[-1]

    def child(source, turn, row, gain):
        real, imag = (
            source[half * SPAN : (half + 1) * SPAN].astype(jnp.float32).reshape(BAND, width) for half in range(2)
        )
        scale = jnp.concatenate([gain] * (width // LANES), axis=1)
        return turned(real, imag, scale * turn[row : row + 1, :], scale * turn[row + 1 : row + 2, :])

    def merge(left, right, table):
        merged = jnp.dot(table[...], joined(left, right), preferred_element_type=jnp.float32)
        return merged[:, :width], merged[:, width:]

    own, one, two, three = images
    near_turn, far_turn, last_turn = turns
    near = merge(child(own, near_turn, 0, gains[0:1]), child(one, near_turn, 2, gains[1:2]), tables[0])
    near = turned(*near, last_turn[0:1, :], last_turn[1:2, :])
    far = merge(child(two, far_turn, 0, gains[2:3]), child(three, far_turn, 2, gains[3:4]), tables[1])
    far = turned(*far, last_turn[2:3, :], last_turn[3:4, :])
    return joined(near, far)


def merge_kernel(cells, *refs):
    images, tables, turns, energies = refs[0:4], refs[4:7], refs[7:10], refs[10:14]
    result, gains = refs[14:16]

    def unsealed(tail):
        terms = tail[0].astype(jnp.float32)
        return terms[0:1] + terms[1:2] + terms[2:3]

    energy = jnp.concatenate([energies[0][...]] + [unsealed(tail) for tail in energies[1:]])
    gains[...] = lax.rsqrt(energy / cells + 1e-06)
    both = first_merges(images, tables, turns, gains[...])
    merged = jnp.dot(tables[2][...], both, preferred_element_type=jnp.float32)
    width = result.shape[-1]
    result[0, 0] = merged[:, :width].astype(jnp.bfloat16)
    result[0, 1] = merged[:, width:].astype(jnp.bfloat16)


def merge_cost(width, beams):
    flops = 8 * width * BAND * (2 * BAND + beams)
    return pl.CostEstimate(flops=flops, bytes_accessed=8192 * width, transcendentals=0)


def merge_first(images, tables, turns, energy, tails, cells, shape):
    width = images[1].shape[-1]
    beams = shape[2]
    in_specs = [pl.BlockSpec((image.shape[0], TILE, BLOCK), lambda i: (0, 0, i)) for image in images]
    in_specs += [pl.BlockSpec(t.shape, lambda i: (0, 0)) for t in tables]
    in_specs += [pl.BlockSpec((t.shape[0], BLOCK), lambda i: (0, i)) for t in turns]
    in_specs += [pl.BlockSpec((1, LANES), lambda i: (0, 0))]
    in_specs += [pl.BlockSpec((1, TILE, LANES), lambda i: (2 * SPAN, 0, 0)) for tail in tails]
    return pl.pallas_call(
        functools.partial(merge_kernel, cells),
        grid=(width // BLOCK,),
        out_shape=[jax.ShapeDtypeStruct(shape, jnp.bfloat16), jax.ShapeDtypeStruct((GROUP, LANES), jnp.float32)],
        in_specs=in_specs,
        out_specs=[
            pl.BlockSpec((1, 2, beams, BLOCK), lambda i: (0, 0, 0, i)),
            pl.BlockSpec((GROUP, LANES), lambda i: (0, 0)),
        ],
        compiler_params=pltpu.CompilerParams(vmem_limit_bytes=16 * 2**20),
        cost_estimate=merge_cost(width, beams),
        name="merge",
    )(*images, *tables, *turns, energy, *tails)


def finish_kernel(at, skip, *refs):
    images, tables, turns, gains = refs[0:4], refs[4:7], refs[7:10], refs[10]
    result, buffer, sems = refs[12:15]
    width = buffer.shape[-1]
    bins = slice(at, at + width)
    own, one, two, three = images
    cut = [own[:, :, skip : skip + width], one[...], two[:, :, skip : skip + width], three[...]]
    both = first_merges(cut, tables, [turn[:, bins] for turn in turns], gains[...])
    copies = []
    for k, row in enumerate(range(0, buffer.shape[1], OUT_ROWS)):
        rows = slice(row, row + OUT_ROWS)
        merged = jnp.dot(tables[2][rows, :], both, preferred_element_type=jnp.float32)
        for half in range(2):
            buffer[half, rows] = merged[:, half * width : (half + 1) * width].astype(jnp.bfloat16)
        copies.append(pltpu.make_async_copy(buffer.at[:, rows], result.at[0, :, rows, bins], sems.at[k]))
        copies[-1].start()
    for copy in copies:
        copy.wait()


def finish(prior, at, images, tables, turns, gains):
    width = images[1].shape[-1]
    beams = prior.shape[2]
    operands = [*images, *tables, *turns, gains]
    return pl.pallas_call(
        functools.partial(finish_kernel, at, at % FAR_PARTS[0]),
        out_shape=jax.ShapeDtypeStruct(prior.shape, prior.dtype),
        in_specs=[pl.BlockSpec(memory_space=pltpu.VMEM)] * len(operands) + [pl.BlockSpec(memory_space=pl.ANY)],
        out_specs=pl.BlockSpec(memory_space=pl.ANY),
        scratch_shapes=[pltpu.VMEM((2, beams, width), prior.dtype), pltpu.SemaphoreType.DMA((beams // OUT_ROWS,))],
        input_output_aliases={len(operands): 0},
        compiler_params=pltpu.CompilerParams(vmem_limit_bytes=16 * 2**20),
        cost_estimate=merge_cost(width, beams),
        name="finish",
    )(*operands, prior)


def shards(polar, autofocus, offsets, weights):
    beams, bins = polar.shape[2], polar.shape[3]
    cells = 2 * beams * lax.axis_size("sec") * bins // 2
    rows = polar.reshape(2, beams // TILE, TILE, bins)
    low, _ = place_bits()

    first = lax.dynamic_slice(rows, (0, low * STEP, 0, 0), (2, SPAN, TILE, FAR_PARTS[0]))
    first = first.reshape(2 * SPAN, TILE, FAR_PARTS[0])
    far = [partner(first, 2)]
    rows, first = lax.optimization_barrier((rows, first))
    second, *near, energy, near_data, last_data = prepare(rows, (weights, offsets, autofocus))
    energy = lax.psum(energy, "sec")
    second, near[0] = seal(second, near[0], energy)
    far.append(partner(second, 2))
    near_table, near_turn = make_table(BAND, near_data, beams)
    last_table, last_turn = make_table(beams, last_data, beams)
    near[1], far[0], near_table, last_table = lax.optimization_barrier((near[1], far[0], near_table, last_table))
    one, three = ([partner(part, flip) for part in near[:2]] for flip in (1, 3))
    near[2], one[0], three[0] = lax.optimization_barrier((near[2], one[0], three[0]))
    one.append(partner(near[2], 1))
    three.append(partner(near[2], 3))
    far_table, far_turn = make_table(BAND, far[1], beams)

    tables = [near_table, far_table, last_table]
    turns = [near_turn, far_turn, last_turn]
    own = [first, second]
    images = [first, one[0], far[0], three[0]]
    merged, gains = merge_first(images, tables, turns, energy, [one[0], far[1], three[0]], cells, polar.shape)
    at = NEAR_PARTS[0]
    for i in (1, 2):
        k = at // FAR_PARTS[0]
        merged = finish(merged, at, [own[k], one[i], far[k], three[i]], tables, turns, gains)
        at += NEAR_PARTS[i]
    return merged


def solution(mesh):
    ring = Mesh(mesh.devices.reshape(-1, GROUP, mesh.devices.shape[1]), ("rest", "x", "sec"))
    placed = (
        P(("rest", "x"), None, "sec", None),
        P(None, None, ("rest", "x"), None),
        P(None, None, ("rest", "x"), "sec"),
        P(None, None, ("rest", "x"), None, "sec"),
    )
    return jax.shard_map(
        shards, mesh=ring, in_specs=placed, out_specs=P(("rest", "x"), None, "sec", None), check_vma=False
    )
```

time: 132 us -> 63.1 us (0.48)
  the two profiles are of different devices: /device:TPU:1 before, /device:TPU:2 now
where the time goes in v1:
time: 63.1 us; the launch traced here: 62.5 us
  starting transfers between devices  31.4 us (50%)
  Pallas kernels  15.6 us (25%)
  blocking collectives  7.48 us (12%)
  waiting for transfers between devices  4.28 us (7%)
  local copies, waits for them, and re-layouts  3.45 us (5%)
    ppermute x8, starting transfers between devices, partner(): return lax.ppermute(value, 'x', [(i, i ^ flip) for i in range(GROUP)])  31.4 us
    psum x1, blocking collectives, shards(): energy = lax.psum(energy, 'sec')  7.48 us
    pallas_call x3, Pallas kernels, make_table(): pl.pallas_call(table_kernel, out_shape=[jax.ShapeDtypeStruct(s, jnp.float...  6.58 us
    ppermute x8, waiting for transfers between devices, partner(): return lax.ppermute(value, 'x', [(i, i ^ flip) for i in range(GROUP)])  4.28 us
    pallas_call x2, Pallas kernels, finish(): pl.pallas_call(functools.partial(finish_kernel, at, at % FAR_PARTS[0]), o...  3.99 us
    pallas_call x1, Pallas kernels, merge_first(): pl.pallas_call(functools.partial(merge_kernel, cells), grid=(width // BLO...  3.26 us
    unnamed x6, local copies, waits for them, and re-layouts  2.25 us
    pallas_call x1, Pallas kernels, prepare(): pl.pallas_call(prepare_kernel, grid=(1,), out_shape=shapes, in_specs=[*se...  1.72 us
  transfers between devices with their start and end apart: 8, of which 2 were waited for; matrix products, arithmetic and copies ran while one was open for 0% of the time, Pallas kernels for 22%

profile of v1, /device:TPU:2, one launch (start us, length us, event | category | flops | bytes accessed | tf_op | source)
XLA Modules:
  0.0 62.5 jit_solution(140263603632353388)
XLA Ops:
  0.0 1.2 %constant_dynamic-slice_fusion = bf16[2,33,8,768]{3,2,1,0:T(8,128)(2,1)S(1)} fusion(bf16[2,64,8,1024]{3,2,1,0:T(8,128)(2,1)} %bitcast.5, s32[]{:T(128)S(6)} %select_n.11), kind=kLoop, calls=%fused_computation | loop fusion | bytes 1622020 | tf_op jit(solution)/shard_map/dynamic_slice | solution.py:349
  1.2 4.0 %collective-permute-start.5 = (bf16[66,8,768]{2,1,0:T(8,128)(2,1)S(1)}, bf16[66,8,768]{2,1,0:T(8,128)(2,1)S(1)}, u32[]{:S(2)}, u32[]{:S(2)}) collective-permute-start(bf16[66,8,768]{2,1,0:T(8,128)(2,1)S(1)} %bitcast.2), channel_id=1, source_target_pairs={{0,8},{4,12},{8,0},{12,4},{1,9},{5,13},{9,1},{13,5},{2,10},{6,14},... | collective-permute-start | bytes 2433032 | tf_op jit(solution)/shard_map/ppermute | solution.py:29
  5.2 0.0 copy-start
  5.3 0.8 %copy-done = f32[2,2,1,8,512]{4,3,2,1,0:T(8,128)S(1)} copy-done((f32[2,2,1,8,512]{4,3,2,1,0:T(8,128)S(1)}, f32[2,2,1,8,512]{4,3,2,1,0:T(8,128)}, u32[]{:S(2)}) %copy-start) | copy-done | bytes 65560
  6.1 0.0 copy-start.1
  6.1 0.7 %copy-done.1 = f32[2,2,1,1024]{3,2,1,0:T(1,128)S(1)} copy-done((f32[2,2,1,1024]{3,2,1,0:T(1,128)S(1)}, f32[2,2,1,1024]{3,2,1,0:T(1,128)}, u32[]{:S(2)}) %copy-start.1) | copy-done | bytes 16408
  6.8 0.0 copy-start.2
  6.8 0.7 %copy-done.2 = s32[2,2,1,512]{3,2,1,0:T(1,128)S(1)} copy-done((s32[2,2,1,512]{3,2,1,0:T(1,128)S(1)}, s32[2,2,1,512]{3,2,1,0:T(1,128)}, u32[]{:S(2)}) %copy-start.2) | copy-done | bytes 8216
  7.5 1.7 %prepare.1 = (bf16[75,8,256]{2,1,0:T(8,128)(2,1)S(1)}, bf16[67,8,512]{2,1,0:T(8,128)(2,1)S(1)}, bf16[66,8,256]{2,1,0:T(8,128)(2,1)S(1)}, bf16[66,8,256]{2,1,0:T(...) custom-call(f32[2,2,1,8,512]{4,3,2,1,0:T(8,128)S(1)} %copy-done, ...), custom_call_target="tpu_custom_call" | custom-call | flops 1081344 | bytes 4000000 | tf_op jit(solution)/shard_map/prepare/pallas_call | solution.py:119
  9.2 7.5 %psum.7.energy.refs_10_ = f32[1,128]{1,0:T(1,128)S(1)} all-reduce(f32[1,128]{1,0:T(1,128)S(1)} %get-tuple-element.34), channel_id=1, replica_groups=mesh['rest'=32,'x'=4,'sec'=4] {'sec'}, use_global_device_ids=true, to_apply=%region_0.1 | all-reduce | flops 128 | bytes 1024 | tf_op jit(solution)/shard_map/psum | solution.py:354
  16.8 4.2 %collective-permute-start = (bf16[67,8,512]{2,1,0:T(8,128)(2,1)S(1)}, bf16[67,8,512]{2,1,0:T(8,128)(2,1)S(1)}, u32[]{:S(2)}, u32[]{:S(2)}) collective-permute-start(bf16[67,8,512]{2,1,0:T(8,128)(2,1)S(1)} %get-tuple-element.37), channel_id=1, source_target_pairs={{0,4},{4,0},{8,12},{12,8},{1,5},{5,1},{9,13},{13,9},{2,6},{6,2},{1... | collective-permute-start | bytes 1646600 | tf_op jit(solution)/shard_map/ppermute | solution.py:29
  21.0 3.4 %collective-permute-start.1 = (bf16[67,8,512]{2,1,0:T(8,128)(2,1)S(1)}, bf16[67,8,512]{2,1,0:T(8,128)(2,1)S(1)}, u32[]{:S(2)}, u32[]{:S(2)}) collective-permute-start(bf16[67,8,512]{2,1,0:T(8,128)(2,1)S(1)} %get-tuple-element.37), channel_id=1, source_target_pairs={{0,12},{4,8},{8,4},{12,0},{1,13},{5,9},{9,5},{13,1},{2,14},{6,10},... | collective-permute-start | bytes 1646600 | tf_op jit(solution)/shard_map/ppermute | solution.py:29
  24.3 3.4 %collective-permute-start.3 = (bf16[75,8,256]{2,1,0:T(8,128)(2,1)S(1)}, bf16[75,8,256]{2,1,0:T(8,128)(2,1)S(1)}, u32[]{:S(2)}, u32[]{:S(2)}) collective-permute-start(bf16[75,8,256]{2,1,0:T(8,128)(2,1)S(1)} %get-tuple-element.35.refs_0_), channel_id=1, source_target_pairs={{0,8},{4,12},{8,0},{12,4},{1,9},{5,13},{9,1},{13,5},{2,10},{6,14},... | collective-permute-start | bytes 921608 | tf_op jit(solution)/shard_map/ppermute | solution.py:29
  27.7 2.9 %table.4 = (f32[512,528]{1,0:T(8,128)S(1)}, f32[4,1024]{1,0:T(4,128)S(1)}) custom-call(bf16[2,8,1024]{2,1,0:T(8,128)(2,1)S(1)} %get-tuple-element.42.data), custom_call_target="tpu_custom_call" | custom-call | flops 6144000 | bytes 2097152 | tf_op jit(solution)/shard_map/table/pallas_call | solution.py:214
  30.6 0.1 convert_element_type.10.refs_6_
  30.7 1.8 %table.3 = (f32[264,528]{1,0:T(8,128)S(1)}, f32[4,1024]{1,0:T(4,128)S(1)}) custom-call(bf16[2,8,1024]{2,1,0:T(8,128)(2,1)S(1)} %get-tuple-element.40.data), custom_call_target="tpu_custom_call" | custom-call | flops 3168000 | bytes 1081344 | tf_op jit(solution)/shard_map/table/pallas_call | solution.py:214
  32.6 0.0 collective-permute-done.5.refs_2_
  32.6 3.1 %collective-permute-start.6 = (bf16[66,8,256]{2,1,0:T(8,128)(2,1)S(1)}, bf16[66,8,256]{2,1,0:T(8,128)(2,1)S(1)}, u32[]{:S(2)}, u32[]{:S(2)}) collective-permute-start(bf16[66,8,256]{2,1,0:T(8,128)(2,1)S(1)} %get-tuple-element.55), channel_id=1, source_target_pairs={{0,4},{4,0},{8,12},{12,8},{1,5},{5,1},{9,13},{13,9},{2,6},{6,2},{1... | collective-permute-start | bytes 811016 | tf_op jit(solution)/shard_map/ppermute | solution.py:29
  35.7 3.4 %collective-permute-start.7 = (bf16[66,8,256]{2,1,0:T(8,128)(2,1)S(1)}, bf16[66,8,256]{2,1,0:T(8,128)(2,1)S(1)}, u32[]{:S(2)}, u32[]{:S(2)}) collective-permute-start(bf16[66,8,256]{2,1,0:T(8,128)(2,1)S(1)} %get-tuple-element.55), channel_id=1, source_target_pairs={{0,12},{4,8},{8,4},{12,0},{1,13},{5,9},{9,5},{13,1},{2,14},{6,10},... | collective-permute-start | bytes 811016 | tf_op jit(solution)/shard_map/ppermute | solution.py:29
  39.1 0.1 collective-permute-done.refs_1_.refs_11_
  39.2 4.1 %collective-permute-done.1.refs_3_.refs_13_ = bf16[67,8,512]{2,1,0:T(8,128)(2,1)S(1)} collective-permute-done((bf16[67,8,512]{2,1,0:T(8,128)(2,1)S(1)}, bf16[67,8,512]{2,1,0:T(8,128)(2,1)S(1)}, u32[]{:S(2)}, u32[]{:S(2)}) %collective-permute-start.1) | collective-permute-done | bytes 548896 | tf_op jit(solution)/shard_map/ppermute | solution.py:29
  43.4 5.4 %collective-permute-start.2 = (bf16[66,8,256]{2,1,0:T(8,128)(2,1)S(1)}, bf16[66,8,256]{2,1,0:T(8,128)(2,1)S(1)}, u32[]{:S(2)}, u32[]{:S(2)}) collective-permute-start(bf16[66,8,256]{2,1,0:T(8,128)(2,1)S(1)} %get-tuple-element.38), channel_id=1, source_target_pairs={{0,4},{4,0},{8,12},{12,8},{1,5},{5,1},{9,13},{13,9},{2,6},{6,2},{1... | collective-permute-start | bytes 811016 | tf_op jit(solution)/shard_map/ppermute | solution.py:29
  48.8 4.5 %collective-permute-start.4 = (bf16[66,8,256]{2,1,0:T(8,128)(2,1)S(1)}, bf16[66,8,256]{2,1,0:T(8,128)(2,1)S(1)}, u32[]{:S(2)}, u32[]{:S(2)}) collective-permute-start(bf16[66,8,256]{2,1,0:T(8,128)(2,1)S(1)} %get-tuple-element.38), channel_id=1, source_target_pairs={{0,12},{4,8},{8,4},{12,0},{1,13},{5,9},{9,5},{13,1},{2,14},{6,10},... | collective-permute-start | bytes 811016 | tf_op jit(solution)/shard_map/ppermute | solution.py:29
  53.3 0.0 collective-permute-done.3.data.refs_12_.refs_2_
  53.3 1.8 %table.5 = (f32[264,528]{1,0:T(8,128)S(1)}, f32[4,1024]{1,0:T(4,128)S(1)}) custom-call(bf16[75,8,256]{2,1,0:T(8,128)(2,1)S(1)} %collective-permute-done.3.data.refs_12_.refs_2_), custom_call_target="tpu_custom_call" | custom-call | flops 3168000 | bytes 1081344 | tf_op jit(solution)/shard_map/table/pallas_call | solution.py:214
  55.2 3.3 %merge.1 = (bf16[1,2,512,1024]{3,2,1,0:T(8,128)(2,1)}, f32[4,128]{1,0:T(4,128)S(1)}) custom-call(bf16[66,8,768]{2,1,0:T(8,128)(2,1)S(1)} %bitcast.3, bf16[67,8,512]{2,1,0:T(8,128)(2,1)S(1)} %collective-permute-done.refs_1_.refs_11_, bf16[66,8,768]{2,1,0:T(8,128)(2,1)S(1)} %collective-permute-done.5.refs_2_, ...), custom_call_target="tpu_custom_call" | custom-call | flops 1124597760 | bytes 4194304 | tf_op jit(solution)/shard_map/merge/pallas_call | solution.py:291
  58.5 0.0 collective-permute-done.6.refs_1_
  58.5 0.0 collective-permute-done.7.refs_3_
  58.5 2.0 %finish.2.refs_11_ = bf16[1,2,512,1024]{3,2,1,0:T(8,128)(2,1)} custom-call(bf16[66,8,768]{2,1,0:T(8,128)(2,1)S(1)} %bitcast.4, bf16[66,8,256]{2,1,0:T(8,128)(2,1)S(1)} %collective-permute-done.6.refs_1_, bf16[66,8,768]{2,1,0:T(8,128)(2,1)S(1)} %collective-permute-done.5.refs_2_, ...), custom_call_target="tpu_custom_call", output_to_operand_aliasing={{}: (11, {})} | custom-call | flops 562298880 | bytes 2097152 | tf_op jit(solution)/shard_map/finish/pallas_call | solution.py:330
  60.5 0.0 collective-permute-done.2.refs_1_
  60.5 0.0 collective-permute-done.4.refs_3_
  60.5 2.0 %finish.3 = bf16[1,2,512,1024]{3,2,1,0:T(8,128)(2,1)} custom-call(bf16[75,8,256]{2,1,0:T(8,128)(2,1)S(1)} %get-tuple-element.35.refs_0_, bf16[66,8,256]{2,1,0:T(8,128)(2,1)S(1)} %collective-permute-done.2.refs_1_, bf16[75,8,256]{2,1,0:T(8,128)(2,1)S(1)} %collective-permute-done.3.data.refs_12_.refs_2_, ...), custom_call_target="tpu_custom_call", output_to_operand_aliasing={{}: (11, {})} | custom-call | flops 562298880 | bytes 2097152 | tf_op jit(solution)/shard_map/finish/pallas_call | solution.py:330
  (3 shorter events, 0.1 us)
Async XLA Ops:
  1.2 31.4 %collective-permute-start.5 = (bf16[66,8,768]{2,1,0:T(8,128)(2,1)S(1)}, bf16[66,8,768]{2,1,0:T(8,128)(2,1)S(1)}, u32[]{:S(2)}, u32[]{:S(2)}) collective-permute-start(bf16[66,8,768]{2,1,0:T(8,128)(2,1)S(1)} %bitcast.2), channel_id=1, source_target_pairs={{0,8},{4,12},{8,0},{12,4},{1,9},{5,13},{9,1},{13,5},{2,10},{6,14},... | collective-permute-start | bytes 2433032 | tf_op jit(solution)/shard_map/ppermute | solution.py:29
  5.2 0.8 %copy-start = (f32[2,2,1,8,512]{4,3,2,1,0:T(8,128)S(1)}, f32[2,2,1,8,512]{4,3,2,1,0:T(8,128)}, u32[]{:S(2)}) copy-start(f32[2,2,1,8,512]{4,3,2,1,0:T(8,128)} %refs_3_.1) | copy-start | bytes 196612
  6.1 0.7 %copy-start.1 = (f32[2,2,1,1024]{3,2,1,0:T(1,128)S(1)}, f32[2,2,1,1024]{3,2,1,0:T(1,128)}, u32[]{:S(2)}) copy-start(f32[2,2,1,1024]{3,2,1,0:T(1,128)} %refs_5_.1) | copy-start | bytes 49156
  6.8 0.7 %copy-start.2 = (s32[2,2,1,512]{3,2,1,0:T(1,128)S(1)}, s32[2,2,1,512]{3,2,1,0:T(1,128)}, u32[]{:S(2)}) copy-start(s32[2,2,1,512]{3,2,1,0:T(1,128)} %refs_4_.1) | copy-start | bytes 24580
  16.8 22.4 %collective-permute-start = (bf16[67,8,512]{2,1,0:T(8,128)(2,1)S(1)}, bf16[67,8,512]{2,1,0:T(8,128)(2,1)S(1)}, u32[]{:S(2)}, u32[]{:S(2)}) collective-permute-start(bf16[67,8,512]{2,1,0:T(8,128)(2,1)S(1)} %get-tuple-element.37), channel_id=1, source_target_pairs={{0,4},{4,0},{8,12},{12,8},{1,5},{5,1},{9,13},{13,9},{2,6},{6,2},{1... | collective-permute-start | bytes 1646600 | tf_op jit(solution)/shard_map/ppermute | solution.py:29
  21.0 22.4 %collective-permute-start.1 = (bf16[67,8,512]{2,1,0:T(8,128)(2,1)S(1)}, bf16[67,8,512]{2,1,0:T(8,128)(2,1)S(1)}, u32[]{:S(2)}, u32[]{:S(2)}) collective-permute-start(bf16[67,8,512]{2,1,0:T(8,128)(2,1)S(1)} %get-tuple-element.37), channel_id=1, source_target_pairs={{0,12},{4,8},{8,4},{12,0},{1,13},{5,9},{9,5},{13,1},{2,14},{6,10},... | collective-permute-start | bytes 1646600 | tf_op jit(solution)/shard_map/ppermute | solution.py:29
  24.3 29.0 %collective-permute-start.3 = (bf16[75,8,256]{2,1,0:T(8,128)(2,1)S(1)}, bf16[75,8,256]{2,1,0:T(8,128)(2,1)S(1)}, u32[]{:S(2)}, u32[]{:S(2)}) collective-permute-start(bf16[75,8,256]{2,1,0:T(8,128)(2,1)S(1)} %get-tuple-element.35.refs_0_), channel_id=1, source_target_pairs={{0,8},{4,12},{8,0},{12,4},{1,9},{5,13},{9,1},{13,5},{2,10},{6,14},... | collective-permute-start | bytes 921608 | tf_op jit(solution)/shard_map/ppermute | solution.py:29
  32.6 25.9 %collective-permute-start.6 = (bf16[66,8,256]{2,1,0:T(8,128)(2,1)S(1)}, bf16[66,8,256]{2,1,0:T(8,128)(2,1)S(1)}, u32[]{:S(2)}, u32[]{:S(2)}) collective-permute-start(bf16[66,8,256]{2,1,0:T(8,128)(2,1)S(1)} %get-tuple-element.55), channel_id=1, source_target_pairs={{0,4},{4,0},{8,12},{12,8},{1,5},{5,1},{9,13},{13,9},{2,6},{6,2},{1... | collective-permute-start | bytes 811016 | tf_op jit(solution)/shard_map/ppermute | solution.py:29
  35.7 22.8 %collective-permute-start.7 = (bf16[66,8,256]{2,1,0:T(8,128)(2,1)S(1)}, bf16[66,8,256]{2,1,0:T(8,128)(2,1)S(1)}, u32[]{:S(2)}, u32[]{:S(2)}) collective-permute-start(bf16[66,8,256]{2,1,0:T(8,128)(2,1)S(1)} %get-tuple-element.55), channel_id=1, source_target_pairs={{0,12},{4,8},{8,4},{12,0},{1,13},{5,9},{9,5},{13,1},{2,14},{6,10},... | collective-permute-start | bytes 811016 | tf_op jit(solution)/shard_map/ppermute | solution.py:29
  43.4 17.2 %collective-permute-start.2 = (bf16[66,8,256]{2,1,0:T(8,128)(2,1)S(1)}, bf16[66,8,256]{2,1,0:T(8,128)(2,1)S(1)}, u32[]{:S(2)}, u32[]{:S(2)}) collective-permute-start(bf16[66,8,256]{2,1,0:T(8,128)(2,1)S(1)} %get-tuple-element.38), channel_id=1, source_target_pairs={{0,4},{4,0},{8,12},{12,8},{1,5},{5,1},{9,13},{13,9},{2,6},{6,2},{1... | collective-permute-start | bytes 811016 | tf_op jit(solution)/shard_map/ppermute | solution.py:29
  48.8 11.7 %collective-permute-start.4 = (bf16[66,8,256]{2,1,0:T(8,128)(2,1)S(1)}, bf16[66,8,256]{2,1,0:T(8,128)(2,1)S(1)}, u32[]{:S(2)}, u32[]{:S(2)}) collective-permute-start(bf16[66,8,256]{2,1,0:T(8,128)(2,1)S(1)} %get-tuple-element.38), channel_id=1, source_target_pairs={{0,12},{4,8},{8,4},{12,0},{1,13},{5,9},{9,5},{13,1},{2,14},{6,10},... | collective-permute-start | bytes 811016 | tf_op jit(solution)/shard_map/ppermute | solution.py:29

commit v2 on v1

--- a/solution.py
+++ b/solution.py
@@ -19,7 +19,7 @@
 BLOCK = 256
 OUT_ROWS = 256
 FAR_PARTS = (768, 256)
-NEAR_PARTS = (512, 256, 256)
+NEAR_PARTS = (768, 256)
 DATA_TILES = 8
 PIECES = 4
 TERMS = 3
@@ -65,6 +65,33 @@
     return [
         jnp.concatenate([data[at + i * each + k].astype(jnp.float32) for k in range(each)], axis=1) for i in range(2)
     ]
+
+
+def cut_kernel(rows, result, sems):
+    low, _ = place_bits()
+    copies = []
+    for half in range(2):
+        for i in range(PIECES):
+            at, end = SPAN * i // PIECES, SPAN * (i + 1) // PIECES
+            source = rows.at[half, pl.ds(low * STEP + at, end - at), :, 0 : result.shape[-1]]
+            target = result.at[pl.ds(half * SPAN + at, end - at)]
+            copies.append(pltpu.make_async_copy(source, target, sems.at[len(copies)]))
+            copies[-1].start()
+    for copy in copies:
+        copy.wait()
+
+
+def cut(rows):
+    return pl.pallas_call(
+        cut_kernel,
+        out_shape=jax.ShapeDtypeStruct((2 * SPAN, TILE, FAR_PARTS[0]), rows.dtype),
+        in_specs=[pl.BlockSpec(memory_space=pl.ANY)],
+        out_specs=pl.BlockSpec(memory_space=pltpu.VMEM),
+        scratch_shapes=[pltpu.SemaphoreType.DMA((2 * PIECES,))],
+        compiler_params=pltpu.CompilerParams(vmem_limit_bytes=52 * 2**20),
+        cost_estimate=pl.CostEstimate(flops=0, bytes_accessed=1_600_000, transcendentals=0),
+        name="cut",
+    )(rows)
 
 
 def section_specs(section, *arrays):
@@ -344,10 +371,8 @@
     beams, bins = polar.shape[2], polar.shape[3]
     cells = 2 * beams * lax.axis_size("sec") * bins // 2
     rows = polar.reshape(2, beams // TILE, TILE, bins)
-    low, _ = place_bits()
-
-    first = lax.dynamic_slice(rows, (0, low * STEP, 0, 0), (2, SPAN, TILE, FAR_PARTS[0]))
-    first = first.reshape(2 * SPAN, TILE, FAR_PARTS[0])
+
+    first = cut(rows)
     far = [partner(first, 2)]
     rows, first = lax.optimization_barrier((rows, first))
     second, *near, energy, near_data, last_data = prepare(rows, (weights, offsets, autofocus))
@@ -357,23 +382,14 @@
     near_table, near_turn = make_table(BAND, near_data, beams)
     last_table, last_turn = make_table(beams, last_data, beams)
     near[1], far[0], near_table, last_table = lax.optimization_barrier((near[1], far[0], near_table, last_table))
-    one, three = ([partner(part, flip) for part in near[:2]] for flip in (1, 3))
-    near[2], one[0], three[0] = lax.optimization_barrier((near[2], one[0], three[0]))
-    one.append(partner(near[2], 1))
-    three.append(partner(near[2], 3))
+    one, three = ([partner(part, flip) for part in near] for flip in (1, 3))
     far_table, far_turn = make_table(BAND, far[1], beams)
 
     tables = [near_table, far_table, last_table]
     turns = [near_turn, far_turn, last_turn]
-    own = [first, second]
     images = [first, one[0], far[0], three[0]]
     merged, gains = merge_first(images, tables, turns, energy, [one[0], far[1], three[0]], cells, polar.shape)
-    at = NEAR_PARTS[0]
-    for i in (1, 2):
-        k = at // FAR_PARTS[0]
-        merged = finish(merged, at, [own[k], one[i], far[k], three[i]], tables, turns, gains)
-        at += NEAR_PARTS[i]
-    return merged
+    return finish(merged, NEAR_PARTS[0], [second, one[1], far[1], three[1]], tables, turns, gains)
 
 
 def solution(mesh):

time: 63.1 us -> 58.8 us (0.932)
  the two profiles are of different devices: /device:TPU:2 before, /device:TPU:4 now
where the time goes in v2:
time: 58.8 us; the launch traced here: 58.4 us
  starting transfers between devices  23.2 us (39%)
  Pallas kernels  16.1 us (27%)
  waiting for transfers between devices  12.8 us (22%)
  blocking collectives  5.96 us (10%)
    ppermute x6, starting transfers between devices, partner(): return lax.ppermute(value, 'x', [(i, i ^ flip) for i in range(GROUP)])  23.2 us
    ppermute x6, waiting for transfers between devices, partner(): return lax.ppermute(value, 'x', [(i, i ^ flip) for i in range(GROUP)])  12.8 us
    pallas_call x3, Pallas kernels, make_table(): pl.pallas_call(table_kernel, out_shape=[jax.ShapeDtypeStruct(s, jnp.float...  6.58 us
    psum x1, blocking collectives, shards(): energy = lax.psum(energy, 'sec')  5.96 us
    pallas_call x1, Pallas kernels, merge_first(): pl.pallas_call(functools.partial(merge_kernel, cells), grid=(width // BLO...  4.47 us
    pallas_call x1, Pallas kernels, finish(): pl.pallas_call(functools.partial(finish_kernel, at, at % FAR_PARTS[0]), o...  1.98 us
    pallas_call x1, Pallas kernels, prepare(): pl.pallas_call(prepare_kernel, grid=(1,), out_shape=shapes, in_specs=[*se...  1.73 us
    pallas_call x1, Pallas kernels, cut(): pl.pallas_call(cut_kernel, out_shape=jax.ShapeDtypeStruct((2 * SPAN, TILE...  1.34 us
  transfers between devices with their start and end apart: 6, of which 1 were waited for; matrix products, arithmetic and copies ran while one was open for 0% of the time, Pallas kernels for 22%

profile of v2, /device:TPU:4, one launch (start us, length us, event | category | flops | bytes accessed | tf_op | source)
XLA Modules:
  0.0 58.4 jit_solution(3151059413569909952)
XLA Ops:
  0.0 0.0 copy-start
  0.0 0.0 copy-start.2
  0.0 0.0 copy-start.1
  0.0 1.3 %cut.1.refs_0_ = bf16[66,8,768]{2,1,0:T(8,128)(2,1)S(1)} custom-call(bf16[2,64,8,1024]{3,2,1,0:T(8,128)(2,1)} %bitcast.1), custom_call_target="tpu_custom_call" | custom-call | bytes 1600000 | tf_op jit(solution)/shard_map/cut/pallas_call | solution.py:85
  1.4 7.8 %collective-permute-start = (bf16[66,8,768]{2,1,0:T(8,128)(2,1)S(1)}, bf16[66,8,768]{2,1,0:T(8,128)(2,1)S(1)}, u32[]{:S(2)}, u32[]{:S(2)}) collective-permute-start(bf16[66,8,768]{2,1,0:T(8,128)(2,1)S(1)} %cut.1.refs_0_), channel_id=1, source_target_pairs={{0,8},{4,12},{8,0},{12,4},{1,9},{5,13},{9,1},{13,5},{2,10},{6,14},... | collective-permute-start | bytes 2433032 | tf_op jit(solution)/shard_map/ppermute | solution.py:29
  9.1 0.0 copy-done
  9.1 0.0 copy-done.2
  9.1 0.0 copy-done.1
  9.2 1.7 %prepare.1 = (bf16[75,8,256]{2,1,0:T(8,128)(2,1)S(1)}, bf16[67,8,768]{2,1,0:T(8,128)(2,1)S(1)}, bf16[66,8,256]{2,1,0:T(8,128)(2,1)S(1)}, f32[1,128]{1,0:T(1,128)...) custom-call(f32[2,2,1,8,512]{4,3,2,1,0:T(8,128)S(1)} %copy-done, s32[2,2,1,512]{3,2,1,0:T(1,128)S(1)} %copy-done.2, ...), custom_call_target="tpu_custom_call" | custom-call | flops 1081344 | bytes 4000000 | tf_op jit(solution)/shard_map/prepare/pallas_call | solution.py:146
  10.9 6.0 %psum.7.energy.refs_10_ = f32[1,128]{1,0:T(1,128)S(1)} all-reduce(f32[1,128]{1,0:T(1,128)S(1)} %get-tuple-element.30), channel_id=1, replica_groups=mesh['rest'=32,'x'=4,'sec'=4] {'sec'}, use_global_device_ids=true, to_apply=%region_0.0 | all-reduce | flops 128 | bytes 1024 | tf_op jit(solution)/shard_map/psum | solution.py:379
  16.9 1.9 %collective-permute-start.5 = (bf16[67,8,768]{2,1,0:T(8,128)(2,1)S(1)}, bf16[67,8,768]{2,1,0:T(8,128)(2,1)S(1)}, u32[]{:S(2)}, u32[]{:S(2)}) collective-permute-start(bf16[67,8,768]{2,1,0:T(8,128)(2,1)S(1)} %get-tuple-element.45), channel_id=1, source_target_pairs={{0,12},{4,8},{8,4},{12,0},{1,13},{5,9},{9,5},{13,1},{2,14},{6,10},... | collective-permute-start | bytes 2469896 | tf_op jit(solution)/shard_map/ppermute | solution.py:29
  18.8 3.1 %collective-permute-start.4 = (bf16[67,8,768]{2,1,0:T(8,128)(2,1)S(1)}, bf16[67,8,768]{2,1,0:T(8,128)(2,1)S(1)}, u32[]{:S(2)}, u32[]{:S(2)}) collective-permute-start(bf16[67,8,768]{2,1,0:T(8,128)(2,1)S(1)} %get-tuple-element.45), channel_id=1, source_target_pairs={{0,4},{4,0},{8,12},{12,8},{1,5},{5,1},{9,13},{13,9},{2,6},{6,2},{1... | collective-permute-start | bytes 2469896 | tf_op jit(solution)/shard_map/ppermute | solution.py:29
  21.9 4.2 %collective-permute-start.2 = (bf16[75,8,256]{2,1,0:T(8,128)(2,1)S(1)}, bf16[75,8,256]{2,1,0:T(8,128)(2,1)S(1)}, u32[]{:S(2)}, u32[]{:S(2)}) collective-permute-start(bf16[75,8,256]{2,1,0:T(8,128)(2,1)S(1)} %get-tuple-element.31.refs_0_), channel_id=1, source_target_pairs={{0,8},{4,12},{8,0},{12,4},{1,9},{5,13},{9,1},{13,5},{2,10},{6,14},... | collective-permute-start | bytes 921608 | tf_op jit(solution)/shard_map/ppermute | solution.py:29
  26.1 1.8 %table.3 = (f32[264,528]{1,0:T(8,128)S(1)}, f32[4,1024]{1,0:T(4,128)S(1)}) custom-call(bf16[2,8,1024]{2,1,0:T(8,128)(2,1)S(1)} %get-tuple-element.33.data), custom_call_target="tpu_custom_call" | custom-call | flops 3168000 | bytes 1081344 | tf_op jit(solution)/shard_map/table/pallas_call | solution.py:241
  28.0 2.9 %table.4 = (f32[512,528]{1,0:T(8,128)S(1)}, f32[4,1024]{1,0:T(4,128)S(1)}) custom-call(bf16[2,8,1024]{2,1,0:T(8,128)(2,1)S(1)} %get-tuple-element.35.data), custom_call_target="tpu_custom_call" | custom-call | flops 6144000 | bytes 2097152 | tf_op jit(solution)/shard_map/table/pallas_call | solution.py:241
  31.0 0.1 convert_element_type.10.refs_6_
  31.0 0.0 collective-permute-done.refs_2_
  31.0 1.9 %collective-permute-start.3 = (bf16[66,8,256]{2,1,0:T(8,128)(2,1)S(1)}, bf16[66,8,256]{2,1,0:T(8,128)(2,1)S(1)}, u32[]{:S(2)}, u32[]{:S(2)}) collective-permute-start(bf16[66,8,256]{2,1,0:T(8,128)(2,1)S(1)} %get-tuple-element.37), channel_id=1, source_target_pairs={{0,12},{4,8},{8,4},{12,0},{1,13},{5,9},{9,5},{13,1},{2,14},{6,10},... | collective-permute-start | bytes 811016 | tf_op jit(solution)/shard_map/ppermute | solution.py:29
  33.0 4.3 %collective-permute-start.1 = (bf16[66,8,256]{2,1,0:T(8,128)(2,1)S(1)}, bf16[66,8,256]{2,1,0:T(8,128)(2,1)S(1)}, u32[]{:S(2)}, u32[]{:S(2)}) collective-permute-start(bf16[66,8,256]{2,1,0:T(8,128)(2,1)S(1)} %get-tuple-element.37), channel_id=1, source_target_pairs={{0,4},{4,0},{8,12},{12,8},{1,5},{5,1},{9,13},{13,9},{2,6},{6,2},{1... | collective-permute-start | bytes 811016 | tf_op jit(solution)/shard_map/ppermute | solution.py:29
  37.3 12.8 %collective-permute-done.2.data.refs_12_.refs_2_ = bf16[75,8,256]{2,1,0:T(8,128)(2,1)S(1)} collective-permute-done((bf16[75,8,256]{2,1,0:T(8,128)(2,1)S(1)}, bf16[75,8,256]{2,1,0:T(8,128)(2,1)S(1)}, u32[]{:S(2)}, u32[]{:S(2)}) %collective-permute-start.2) | collective-permute-done | bytes 307232 | tf_op jit(solution)/shard_map/ppermute | solution.py:29
  50.1 1.8 %table.5 = (f32[264,528]{1,0:T(8,128)S(1)}, f32[4,1024]{1,0:T(4,128)S(1)}) custom-call(bf16[75,8,256]{2,1,0:T(8,128)(2,1)S(1)} %collective-permute-done.2.data.refs_12_.refs_2_), custom_call_target="tpu_custom_call" | custom-call | flops 3168000 | bytes 1081344 | tf_op jit(solution)/shard_map/table/pallas_call | solution.py:241
  52.0 0.0 collective-permute-done.5.refs_3_.refs_13_
  52.0 0.0 collective-permute-done.4.refs_1_.refs_11_
  52.0 4.5 %merge.1 = (bf16[1,2,512,1024]{3,2,1,0:T(8,128)(2,1)}, f32[4,128]{1,0:T(4,128)S(1)}) custom-call(bf16[66,8,768]{2,1,0:T(8,128)(2,1)S(1)} %cut.1.refs_0_, bf16[67,8,768]{2,1,0:T(8,128)(2,1)S(1)} %collective-permute-done.4.refs_1_.refs_11_, bf16[66,8,768]{2,1,0:T(8,128)(2,1)S(1)} %collective-permute-done.refs_2_, ...), custom_call_target="tpu_custom_call" | custom-call | flops 1686896640 | bytes 6291456 | tf_op jit(solution)/shard_map/merge/pallas_call | solution.py:318
  56.5 0.0 collective-permute-done.3.refs_3_
  56.5 0.0 collective-permute-done.1.refs_1_
  56.5 2.0 %finish.1 = bf16[1,2,512,1024]{3,2,1,0:T(8,128)(2,1)} custom-call(bf16[75,8,256]{2,1,0:T(8,128)(2,1)S(1)} %get-tuple-element.31.refs_0_, bf16[66,8,256]{2,1,0:T(8,128)(2,1)S(1)} %collective-permute-done.1.refs_1_, bf16[75,8,256]{2,1,0:T(8,128)(2,1)S(1)} %collective-permute-done.2.data.refs_12_.refs_2_, ...), custom_call_target="tpu_custom_call", output_to_operand_aliasing={{}: (11, {})} | custom-call | flops 562298880 | bytes 2097152 | tf_op jit(solution)/shard_map/finish/pallas_call | solution.py:357
  (3 shorter events, 0.1 us)
Async XLA Ops:
  0.0 9.1 %copy-start = (f32[2,2,1,8,512]{4,3,2,1,0:T(8,128)S(1)}, f32[2,2,1,8,512]{4,3,2,1,0:T(8,128)}, u32[]{:S(2)}) copy-start(f32[2,2,1,8,512]{4,3,2,1,0:T(8,128)} %refs_3_.1) | copy-start | bytes 196612
  0.0 9.1 %copy-start.2 = (s32[2,2,1,512]{3,2,1,0:T(1,128)S(1)}, s32[2,2,1,512]{3,2,1,0:T(1,128)}, u32[]{:S(2)}) copy-start(s32[2,2,1,512]{3,2,1,0:T(1,128)} %refs_4_.1) | copy-start | bytes 24580
  0.0 9.1 %copy-start.1 = (f32[2,2,1,1024]{3,2,1,0:T(1,128)S(1)}, f32[2,2,1,1024]{3,2,1,0:T(1,128)}, u32[]{:S(2)}) copy-start(f32[2,2,1,1024]{3,2,1,0:T(1,128)} %refs_5_.1) | copy-start | bytes 49156
  1.4 29.7 %collective-permute-start = (bf16[66,8,768]{2,1,0:T(8,128)(2,1)S(1)}, bf16[66,8,768]{2,1,0:T(8,128)(2,1)S(1)}, u32[]{:S(2)}, u32[]{:S(2)}) collective-permute-start(bf16[66,8,768]{2,1,0:T(8,128)(2,1)S(1)} %cut.1.refs_0_), channel_id=1, source_target_pairs={{0,8},{4,12},{8,0},{12,4},{1,9},{5,13},{9,1},{13,5},{2,10},{6,14},... | collective-permute-start | bytes 2433032 | tf_op jit(solution)/shard_map/ppermute | solution.py:29
  16.9 35.1 %collective-permute-start.5 = (bf16[67,8,768]{2,1,0:T(8,128)(2,1)S(1)}, bf16[67,8,768]{2,1,0:T(8,128)(2,1)S(1)}, u32[]{:S(2)}, u32[]{:S(2)}) collective-permute-start(bf16[67,8,768]{2,1,0:T(8,128)(2,1)S(1)} %get-tuple-element.45), channel_id=1, source_target_pairs={{0,12},{4,8},{8,4},{12,0},{1,13},{5,9},{9,5},{13,1},{2,14},{6,10},... | collective-permute-start | bytes 2469896 | tf_op jit(solution)/shard_map/ppermute | solution.py:29
  18.8 33.1 %collective-permute-start.4 = (bf16[67,8,768]{2,1,0:T(8,128)(2,1)S(1)}, bf16[67,8,768]{2,1,0:T(8,128)(2,1)S(1)}, u32[]{:S(2)}, u32[]{:S(2)}) collective-permute-start(bf16[67,8,768]{2,1,0:T(8,128)(2,1)S(1)} %get-tuple-element.45), channel_id=1, source_target_pairs={{0,4},{4,0},{8,12},{12,8},{1,5},{5,1},{9,13},{13,9},{2,6},{6,2},{1... | collective-permute-start | bytes 2469896 | tf_op jit(solution)/shard_map/ppermute | solution.py:29
  21.9 28.2 %collective-permute-start.2 = (bf16[75,8,256]{2,1,0:T(8,128)(2,1)S(1)}, bf16[75,8,256]{2,1,0:T(8,128)(2,1)S(1)}, u32[]{:S(2)}, u32[]{:S(2)}) collective-permute-start(bf16[75,8,256]{2,1,0:T(8,128)(2,1)S(1)} %get-tuple-element.31.refs_0_), channel_id=1, source_target_pairs={{0,8},{4,12},{8,0},{12,4},{1,9},{5,13},{9,1},{13,5},{2,10},{6,14},... | collective-permute-start | bytes 921608 | tf_op jit(solution)/shard_map/ppermute | solution.py:29
  31.0 25.4 %collective-permute-start.3 = (bf16[66,8,256]{2,1,0:T(8,128)(2,1)S(1)}, bf16[66,8,256]{2,1,0:T(8,128)(2,1)S(1)}, u32[]{:S(2)}, u32[]{:S(2)}) collective-permute-start(bf16[66,8,256]{2,1,0:T(8,128)(2,1)S(1)} %get-tuple-element.37), channel_id=1, source_target_pairs={{0,12},{4,8},{8,4},{12,0},{1,13},{5,9},{9,5},{13,1},{2,14},{6,10},... | collective-permute-start | bytes 811016 | tf_op jit(solution)/shard_map/ppermute | solution.py:29
  33.0 23.5 %collective-permute-start.1 = (bf16[66,8,256]{2,1,0:T(8,128)(2,1)S(1)}, bf16[66,8,256]{2,1,0:T(8,128)(2,1)S(1)}, u32[]{:S(2)}, u32[]{:S(2)}) collective-permute-start(bf16[66,8,256]{2,1,0:T(8,128)(2,1)S(1)} %get-tuple-element.37), channel_id=1, source_target_pairs={{0,4},{4,0},{8,12},{12,8},{1,5},{5,1},{9,13},{13,9},{2,6},{6,2},{1... | collective-permute-start | bytes 811016 | tf_op jit(solution)/shard_map/ppermute | solution.py:29

commit v3 on v2

--- a/solution.py
+++ b/solution.py
@@ -262,72 +262,116 @@
     return jnp.concatenate(both, axis=1)
 
 
-def first_merges(images, tables, turns, gains):
+def first_merge(images, table, turn, last_turn, gains):
     width = images[1].shape[-1]
 
-    def child(source, turn, row, gain):
+    def child(source, row, gain):
         real, imag = (
             source[half * SPAN : (half + 1) * SPAN].astype(jnp.float32).reshape(BAND, width) for half in range(2)
         )
         scale = jnp.concatenate([gain] * (width // LANES), axis=1)
         return turned(real, imag, scale * turn[row : row + 1, :], scale * turn[row + 1 : row + 2, :])
 
-    def merge(left, right, table):
-        merged = jnp.dot(table[...], joined(left, right), preferred_element_type=jnp.float32)
-        return merged[:, :width], merged[:, width:]
-
-    own, one, two, three = images
-    near_turn, far_turn, last_turn = turns
-    near = merge(child(own, near_turn, 0, gains[0:1]), child(one, near_turn, 2, gains[1:2]), tables[0])
-    near = turned(*near, last_turn[0:1, :], last_turn[1:2, :])
-    far = merge(child(two, far_turn, 0, gains[2:3]), child(three, far_turn, 2, gains[3:4]), tables[1])
-    far = turned(*far, last_turn[2:3, :], last_turn[3:4, :])
-    return joined(near, far)
-
-
-def merge_kernel(cells, *refs):
-    images, tables, turns, energies = refs[0:4], refs[4:7], refs[7:10], refs[10:14]
-    result, gains = refs[14:16]
-
-    def unsealed(tail):
-        terms = tail[0].astype(jnp.float32)
-        return terms[0:1] + terms[1:2] + terms[2:3]
-
+    both = joined(child(images[0], 0, gains[0:1]), child(images[1], 2, gains[1:2]))
+    merged = jnp.dot(table[...], both, preferred_element_type=jnp.float32)
+    return turned(merged[:, :width], merged[:, width:], last_turn[0:1, :], last_turn[1:2, :])
+
+
+def unsealed(tail):
+    terms = tail[0].astype(jnp.float32)
+    return terms[0:1] + terms[1:2] + terms[2:3]
+
+
+def gains_of(energies, cells):
     energy = jnp.concatenate([energies[0][...]] + [unsealed(tail) for tail in energies[1:]])
-    gains[...] = lax.rsqrt(energy / cells + 1e-06)
-    both = first_merges(images, tables, turns, gains[...])
-    merged = jnp.dot(tables[2][...], both, preferred_element_type=jnp.float32)
+    return lax.rsqrt(energy / cells + 1e-06)
+
+
+def near_kernel(cells, own, one, table, turn, last_turn, energy, one_tail, result):
+    gains = gains_of([energy, one_tail], cells)
+    real, imag = first_merge((own, one), table, turn, last_turn[0:2, :], gains)
+    result[0] = real
+    result[1] = imag
+
+
+def far_kernel(cells, near, two, three, far_table, last_table, turn, last_turn, *refs):
+    *energies, result, gains = refs
+    gains[...] = gains_of(energies, cells)
+    far = first_merge((two, three), far_table, turn, last_turn[2:4, :], gains[2:4])
+    both = joined((near[0], near[1]), far)
+    merged = jnp.dot(last_table[...], both, preferred_element_type=jnp.float32)
     width = result.shape[-1]
     result[0, 0] = merged[:, :width].astype(jnp.bfloat16)
     result[0, 1] = merged[:, width:].astype(jnp.bfloat16)
 
 
-def merge_cost(width, beams):
-    flops = 8 * width * BAND * (2 * BAND + beams)
-    return pl.CostEstimate(flops=flops, bytes_accessed=8192 * width, transcendentals=0)
-
-
-def merge_first(images, tables, turns, energy, tails, cells, shape):
-    width = images[1].shape[-1]
+def merge_cost(width, rows):
+    flops = 8 * width * BAND * rows
+    return pl.CostEstimate(flops=flops, bytes_accessed=6000 * width, transcendentals=0)
+
+
+def image_spec(image):
+    return pl.BlockSpec((image.shape[0], TILE, BLOCK), lambda i: (0, 0, i))
+
+
+def turn_spec(turn):
+    return pl.BlockSpec((turn.shape[0], BLOCK), lambda i: (0, i))
+
+
+def whole_spec(array):
+    return pl.BlockSpec(array.shape, lambda i: (0,) * len(array.shape))
+
+
+def tail_spec(tail):
+    return pl.BlockSpec((1, TILE, LANES), lambda i: (2 * SPAN, 0, 0))
+
+
+def merge_near(own, one, table, turn, last_turn, energy, cells):
+    width = one.shape[-1]
+    return pl.pallas_call(
+        functools.partial(near_kernel, cells),
+        grid=(width // BLOCK,),
+        out_shape=jax.ShapeDtypeStruct((2, BAND, width), jnp.float32),
+        in_specs=[
+            image_spec(own),
+            image_spec(one),
+            whole_spec(table),
+            turn_spec(turn),
+            turn_spec(last_turn),
+            whole_spec(energy),
+            tail_spec(one),
+        ],
+        out_specs=pl.BlockSpec((2, BAND, BLOCK), lambda i: (0, 0, i)),
+        compiler_params=pltpu.CompilerParams(vmem_limit_bytes=12 * 2**20),
+        cost_estimate=merge_cost(width, BAND),
+        name="near",
+    )(own, one, table, turn, last_turn, energy, one)
+
+
+def merge_far(near, two, three, tables, turns, energy, tails, cells, shape):
+    width = three.shape[-1]
     beams = shape[2]
-    in_specs = [pl.BlockSpec((image.shape[0], TILE, BLOCK), lambda i: (0, 0, i)) for image in images]
-    in_specs += [pl.BlockSpec(t.shape, lambda i: (0, 0)) for t in tables]
-    in_specs += [pl.BlockSpec((t.shape[0], BLOCK), lambda i: (0, i)) for t in turns]
-    in_specs += [pl.BlockSpec((1, LANES), lambda i: (0, 0))]
-    in_specs += [pl.BlockSpec((1, TILE, LANES), lambda i: (2 * SPAN, 0, 0)) for tail in tails]
-    return pl.pallas_call(
-        functools.partial(merge_kernel, cells),
+    return pl.pallas_call(
+        functools.partial(far_kernel, cells),
         grid=(width // BLOCK,),
         out_shape=[jax.ShapeDtypeStruct(shape, jnp.bfloat16), jax.ShapeDtypeStruct((GROUP, LANES), jnp.float32)],
-        in_specs=in_specs,
+        in_specs=[
+            pl.BlockSpec((2, BAND, BLOCK), lambda i: (0, 0, i)),
+            image_spec(two),
+            image_spec(three),
+            *[whole_spec(table) for table in tables],
+            *[turn_spec(turn) for turn in turns],
+            whole_spec(energy),
+            *[tail_spec(tail) for tail in tails],
+        ],
         out_specs=[
             pl.BlockSpec((1, 2, beams, BLOCK), lambda i: (0, 0, 0, i)),
             pl.BlockSpec((GROUP, LANES), lambda i: (0, 0)),
         ],
         compiler_params=pltpu.CompilerParams(vmem_limit_bytes=16 * 2**20),
-        cost_estimate=merge_cost(width, beams),
+        cost_estimate=merge_cost(width, BAND + beams),
         name="merge",
-    )(*images, *tables, *turns, energy, *tails)
+    )(near, two, three, *tables, *turns, energy, *tails)
 
 
 def finish_kernel(at, skip, *refs):
@@ -336,8 +380,10 @@
     width = buffer.shape[-1]
     bins = slice(at, at + width)
     own, one, two, three = images
-    cut = [own[:, :, skip : skip + width], one[...], two[:, :, skip : skip + width], three[...]]
-    both = first_merges(cut, tables, [turn[:, bins] for turn in turns], gains[...])
+    near_turn, far_turn, last_turn = (turn[:, bins] for turn in turns)
+    near = first_merge((own[:, :, skip : skip + width], one), tables[0], near_turn, last_turn[0:2], gains[0:2])
+    far = first_merge((two[:, :, skip : skip + width], three), tables[1], far_turn, last_turn[2:4], gains[2:4])
+    both = joined(near, far)
     copies = []
     for k, row in enumerate(range(0, buffer.shape[1], OUT_ROWS)):
         rows = slice(row, row + OUT_ROWS)
@@ -362,7 +408,7 @@
         scratch_shapes=[pltpu.VMEM((2, beams, width), prior.dtype), pltpu.SemaphoreType.DMA((beams // OUT_ROWS,))],
         input_output_aliases={len(operands): 0},
         compiler_params=pltpu.CompilerParams(vmem_limit_bytes=16 * 2**20),
-        cost_estimate=merge_cost(width, beams),
+        cost_estimate=merge_cost(width, 2 * BAND + beams),
         name="finish",
     )(*operands, prior)
 
@@ -383,12 +429,13 @@
     last_table, last_turn = make_table(beams, last_data, beams)
     near[1], far[0], near_table, last_table = lax.optimization_barrier((near[1], far[0], near_table, last_table))
     one, three = ([partner(part, flip) for part in near] for flip in (1, 3))
+    merged_near = merge_near(first, one[0], near_table, near_turn, last_turn, energy, cells)
+    far[1], merged_near = lax.optimization_barrier((far[1], merged_near))
     far_table, far_turn = make_table(BAND, far[1], beams)
-
-    tables = [near_table, far_table, last_table]
-    turns = [near_turn, far_turn, last_turn]
-    images = [first, one[0], far[0], three[0]]
-    merged, gains = merge_first(images, tables, turns, energy, [one[0], far[1], three[0]], cells, polar.shape)
+    tails = [one[0], far[1], three[0]]
+    tables, turns = [far_table, last_table], [far_turn, last_turn]
+    merged, gains = merge_far(merged_near, far[0], three[0], tables, turns, energy, tails, cells, polar.shape)
+    tables, turns = [near_table, far_table, last_table], [near_turn, far_turn, last_turn]
     return finish(merged, NEAR_PARTS[0], [second, one[1], far[1], three[1]], tables, turns, gains)
 
 

time: 58.8 us -> 59.8 us (1.017)
  waiting for transfers between devices: 12.8 us -> 14.1 us
  starting transfers between devices: 23.2 us -> 22 us
  Pallas kernels: 16.1 us -> 17.1 us
    ppermute x6, waiting for transfers between devices: 12.8 us -> 14.1 us  [partner(): return lax.ppermute(value, 'x', [(i, i ^ flip) for i in range(GROUP)])]
    ppermute x6, starting transfers between devices: 23.2 us -> 22 us  [partner(): return lax.ppermute(value, 'x', [(i, i ^ flip) for i in range(GROUP)])]
    pallas_call x1 -> x2, Pallas kernels: 4.47 us -> 5.44 us  [the longest x1 3.78 us: merge_far(): pl.pallas_call(functools.partial(far_kernel, cells), grid=(width // BLOCK...]
  transfers between devices with their start and end apart: 6 -> 6, of which waited for: 1 -> 2; matrix products, arithmetic and copies ran while one was open for 0% -> 0% of each run, Pallas kernels for 22% -> 23%
where the time goes in v3:
time: 59.8 us; the launch traced here: 59.5 us
  starting transfers between devices  22 us (37%)
  Pallas kernels  17.1 us (29%)
  waiting for transfers between devices  14.1 us (24%)
  blocking collectives  5.96 us (10%)
    ppermute x6, starting transfers between devices, partner(): return lax.ppermute(value, 'x', [(i, i ^ flip) for i in range(GROUP)])  22 us
    ppermute x6, waiting for transfers between devices, partner(): return lax.ppermute(value, 'x', [(i, i ^ flip) for i in range(GROUP)])  14.1 us
    pallas_call x3, Pallas kernels, make_table(): pl.pallas_call(table_kernel, out_shape=[jax.ShapeDtypeStruct(s, jnp.float...  6.58 us
    psum x1, blocking collectives, shards(): energy = lax.psum(energy, 'sec')  5.96 us
    pallas_call x1, Pallas kernels, merge_far(): pl.pallas_call(functools.partial(far_kernel, cells), grid=(width // BLOCK...  3.78 us
    pallas_call x1, Pallas kernels, finish(): pl.pallas_call(functools.partial(finish_kernel, at, at % FAR_PARTS[0]), o...  1.98 us
    pallas_call x1, Pallas kernels, prepare(): pl.pallas_call(prepare_kernel, grid=(1,), out_shape=shapes, in_specs=[*se...  1.73 us
    pallas_call x1, Pallas kernels, merge_near(): pl.pallas_call(functools.partial(near_kernel, cells), grid=(width // BLOC...  1.67 us
  transfers between devices with their start and end apart: 6, of which 2 were waited for; matrix products, arithmetic and copies ran while one was open for 0% of the time, Pallas kernels for 23%

profile of v3, /device:TPU:4, one launch (start us, length us, event | category | flops | bytes accessed | tf_op | source)
XLA Modules:
  0.0 59.5 jit_solution(3110246982335731732)
XLA Ops:
  0.0 0.0 copy-start.1
  0.0 0.0 copy-start.2
  0.0 0.0 copy-start
  0.0 1.3 %cut.1.own = bf16[66,8,768]{2,1,0:T(8,128)(2,1)S(1)} custom-call(bf16[2,64,8,1024]{3,2,1,0:T(8,128)(2,1)} %bitcast.1), custom_call_target="tpu_custom_call" | custom-call | bytes 1600000 | tf_op jit(solution)/shard_map/cut/pallas_call | solution.py:85
  1.4 7.8 %collective-permute-start = (bf16[66,8,768]{2,1,0:T(8,128)(2,1)S(1)}, bf16[66,8,768]{2,1,0:T(8,128)(2,1)S(1)}, u32[]{:S(2)}, u32[]{:S(2)}) collective-permute-start(bf16[66,8,768]{2,1,0:T(8,128)(2,1)S(1)} %cut.1.own), channel_id=1, source_target_pairs={{0,8},{4,12},{8,0},{12,4},{1,9},{5,13},{9,1},{13,5},{2,10},{6,14},... | collective-permute-start | bytes 2433032 | tf_op jit(solution)/shard_map/ppermute | solution.py:29
  9.1 0.0 copy-done.1
  9.1 0.0 copy-done.2
  9.1 0.0 copy-done
  9.2 1.7 %prepare.1 = (bf16[75,8,256]{2,1,0:T(8,128)(2,1)S(1)}, bf16[67,8,768]{2,1,0:T(8,128)(2,1)S(1)}, bf16[66,8,256]{2,1,0:T(8,128)(2,1)S(1)}, f32[1,128]{1,0:T(1,128)...) custom-call(f32[2,2,1,8,512]{4,3,2,1,0:T(8,128)S(1)} %copy-done, s32[2,2,1,512]{3,2,1,0:T(1,128)S(1)} %copy-done.2, ...), custom_call_target="tpu_custom_call" | custom-call | flops 1081344 | bytes 4000000 | tf_op jit(solution)/shard_map/prepare/pallas_call | solution.py:146
  10.9 6.0 %psum.7.energy.refs_0_ = f32[1,128]{1,0:T(1,128)S(1)} all-reduce(f32[1,128]{1,0:T(1,128)S(1)} %get-tuple-element.32), channel_id=1, replica_groups=mesh['rest'=32,'x'=4,'sec'=4] {'sec'}, use_global_device_ids=true, to_apply=%region_0.0 | all-reduce | flops 128 | bytes 1024 | tf_op jit(solution)/shard_map/psum | solution.py:425
  16.9 1.9 %collective-permute-start.3 = (bf16[67,8,768]{2,1,0:T(8,128)(2,1)S(1)}, bf16[67,8,768]{2,1,0:T(8,128)(2,1)S(1)}, u32[]{:S(2)}, u32[]{:S(2)}) collective-permute-start(bf16[67,8,768]{2,1,0:T(8,128)(2,1)S(1)} %get-tuple-element.41), channel_id=1, source_target_pairs={{0,4},{4,0},{8,12},{12,8},{1,5},{5,1},{9,13},{13,9},{2,6},{6,2},{1... | collective-permute-start | bytes 2469896 | tf_op jit(solution)/shard_map/ppermute | solution.py:29
  18.8 2.5 %collective-permute-start.5 = (bf16[67,8,768]{2,1,0:T(8,128)(2,1)S(1)}, bf16[67,8,768]{2,1,0:T(8,128)(2,1)S(1)}, u32[]{:S(2)}, u32[]{:S(2)}) collective-permute-start(bf16[67,8,768]{2,1,0:T(8,128)(2,1)S(1)} %get-tuple-element.41), channel_id=1, source_target_pairs={{0,12},{4,8},{8,4},{12,0},{1,13},{5,9},{9,5},{13,1},{2,14},{6,10},... | collective-permute-start | bytes 2469896 | tf_op jit(solution)/shard_map/ppermute | solution.py:29
  21.3 5.4 %collective-permute-start.2 = (bf16[75,8,256]{2,1,0:T(8,128)(2,1)S(1)}, bf16[75,8,256]{2,1,0:T(8,128)(2,1)S(1)}, u32[]{:S(2)}, u32[]{:S(2)}) collective-permute-start(bf16[75,8,256]{2,1,0:T(8,128)(2,1)S(1)} %get-tuple-element.33.refs_0_), channel_id=1, source_target_pairs={{0,8},{4,12},{8,0},{12,4},{1,9},{5,13},{9,1},{13,5},{2,10},{6,14},... | collective-permute-start | bytes 921608 | tf_op jit(solution)/shard_map/ppermute | solution.py:29
  26.8 2.9 %table.4 = (f32[512,528]{1,0:T(8,128)S(1)}, f32[4,1024]{1,0:T(4,128)S(1)}) custom-call(bf16[2,8,1024]{2,1,0:T(8,128)(2,1)S(1)} %get-tuple-element.37.data), custom_call_target="tpu_custom_call" | custom-call | flops 6144000 | bytes 2097152 | tf_op jit(solution)/shard_map/table/pallas_call | solution.py:241
  29.7 0.1 convert_element_type.10.last_table.refs_6_
  29.7 1.8 %table.3 = (f32[264,528]{1,0:T(8,128)S(1)}, f32[4,1024]{1,0:T(4,128)S(1)}) custom-call(bf16[2,8,1024]{2,1,0:T(8,128)(2,1)S(1)} %get-tuple-element.35.data), custom_call_target="tpu_custom_call" | custom-call | flops 3168000 | bytes 1081344 | tf_op jit(solution)/shard_map/table/pallas_call | solution.py:241
  31.6 0.0 collective-permute-done.two
  31.7 1.9 %collective-permute-start.1 = (bf16[66,8,256]{2,1,0:T(8,128)(2,1)S(1)}, bf16[66,8,256]{2,1,0:T(8,128)(2,1)S(1)}, u32[]{:S(2)}, u32[]{:S(2)}) collective-permute-start(bf16[66,8,256]{2,1,0:T(8,128)(2,1)S(1)} %get-tuple-element.39), channel_id=1, source_target_pairs={{0,4},{4,0},{8,12},{12,8},{1,5},{5,1},{9,13},{13,9},{2,6},{6,2},{1... | collective-permute-start | bytes 811016 | tf_op jit(solution)/shard_map/ppermute | solution.py:29
  33.6 2.5 %collective-permute-start.4 = (bf16[66,8,256]{2,1,0:T(8,128)(2,1)S(1)}, bf16[66,8,256]{2,1,0:T(8,128)(2,1)S(1)}, u32[]{:S(2)}, u32[]{:S(2)}) collective-permute-start(bf16[66,8,256]{2,1,0:T(8,128)(2,1)S(1)} %get-tuple-element.39), channel_id=1, source_target_pairs={{0,12},{4,8},{8,4},{12,0},{1,13},{5,9},{9,5},{13,1},{2,14},{6,10},... | collective-permute-start | bytes 811016 | tf_op jit(solution)/shard_map/ppermute | solution.py:29
  36.1 6.4 %collective-permute-done.3.one.one_tail.refs_1_ = bf16[67,8,768]{2,1,0:T(8,128)(2,1)S(1)} collective-permute-done((bf16[67,8,768]{2,1,0:T(8,128)(2,1)S(1)}, bf16[67,8,768]{2,1,0:T(8,128)(2,1)S(1)}, u32[]{:S(2)}, u32[]{:S(2)}) %collective-permute-start.3) | collective-permute-done | bytes 823328 | tf_op jit(solution)/shard_map/ppermute | solution.py:29
  42.4 1.7 %near.1 = f32[2,264,768]{2,1,0:T(8,128)S(1)} custom-call(bf16[66,8,768]{2,1,0:T(8,128)(2,1)S(1)} %cut.1.own, bf16[67,8,768]{2,1,0:T(8,128)(2,1)S(1)} %collective-permute-done.3.one.one_tail.refs_1_, bf16[264,528]{1,0:T(8,128)(2,1)S(1)} %convert_element_type.9.table.refs_4_, f32[4,1024]{1,0:T(4,128)S(1)} %get-tuple-element.43.turn.refs_7_, ...), custom_call_target="tpu_custom_call" | custom-call | flops 428212224 | bytes 4608000 | tf_op jit(solution)/shard_map/near/pallas_call | solution.py:331
  44.1 7.7 %collective-permute-done.2.data.refs_2_ = bf16[75,8,256]{2,1,0:T(8,128)(2,1)S(1)} collective-permute-done((bf16[75,8,256]{2,1,0:T(8,128)(2,1)S(1)}, bf16[75,8,256]{2,1,0:T(8,128)(2,1)S(1)}, u32[]{:S(2)}, u32[]{:S(2)}) %collective-permute-start.2) | collective-permute-done | bytes 307232 | tf_op jit(solution)/shard_map/ppermute | solution.py:29
  51.8 1.8 %table.5 = (f32[264,528]{1,0:T(8,128)S(1)}, f32[4,1024]{1,0:T(4,128)S(1)}) custom-call(bf16[75,8,256]{2,1,0:T(8,128)(2,1)S(1)} %collective-permute-done.2.data.refs_2_), custom_call_target="tpu_custom_call" | custom-call | flops 3168000 | bytes 1081344 | tf_op jit(solution)/shard_map/table/pallas_call | solution.py:241
  53.7 0.0 collective-permute-done.5.three.refs_3_
  53.7 3.8 %merge.1 = (bf16[1,2,512,1024]{3,2,1,0:T(8,128)(2,1)}, f32[4,128]{1,0:T(4,128)S(1)}) custom-call(f32[2,264,768]{2,1,0:T(8,128)S(1)} %near.1, bf16[66,8,768]{2,1,0:T(8,128)(2,1)S(1)} %collective-permute-done.two, bf16[67,8,768]{2,1,0:T(8,128)(2,1)S(1)} %collective-permute-done.5.three.refs_3_, bf16[264,528]{1,0:T(8,128)(2,1)S(1)} %convert_element_type.11.far_table.refs_5_, ...), custom_call_target="tpu_custom_call" | custom-call | flops 1258684416 | bytes 4608000 | tf_op jit(solution)/shard_map/merge/pallas_call | solution.py:354
  57.5 0.0 collective-permute-done.1.refs_1_
  57.5 0.0 collective-permute-done.4.refs_3_
  57.5 2.0 %finish.1 = bf16[1,2,512,1024]{3,2,1,0:T(8,128)(2,1)} custom-call(bf16[75,8,256]{2,1,0:T(8,128)(2,1)S(1)} %get-tuple-element.33.refs_0_, bf16[66,8,256]{2,1,0:T(8,128)(2,1)S(1)} %collective-permute-done.1.refs_1_, bf16[75,8,256]{2,1,0:T(8,128)(2,1)S(1)} %collective-permute-done.2.data.refs_2_, ...), custom_call_target="tpu_custom_call", output_to_operand_aliasing={{}: (11, {})} | custom-call | flops 562298880 | bytes 1536000 | tf_op jit(solution)/shard_map/finish/pallas_call | solution.py:403
  (3 shorter events, 0.1 us)
Async XLA Ops:
  0.0 9.1 %copy-start.1 = (f32[2,2,1,1024]{3,2,1,0:T(1,128)S(1)}, f32[2,2,1,1024]{3,2,1,0:T(1,128)}, u32[]{:S(2)}) copy-start(f32[2,2,1,1024]{3,2,1,0:T(1,128)} %refs_5_.1) | copy-start | bytes 49156
  0.0 9.1 %copy-start.2 = (s32[2,2,1,512]{3,2,1,0:T(1,128)S(1)}, s32[2,2,1,512]{3,2,1,0:T(1,128)}, u32[]{:S(2)}) copy-start(s32[2,2,1,512]{3,2,1,0:T(1,128)} %refs_4_.1) | copy-start | bytes 24580
  0.0 9.1 %copy-start = (f32[2,2,1,8,512]{4,3,2,1,0:T(8,128)S(1)}, f32[2,2,1,8,512]{4,3,2,1,0:T(8,128)}, u32[]{:S(2)}) copy-start(f32[2,2,1,8,512]{4,3,2,1,0:T(8,128)} %refs_3_.1) | copy-start | bytes 196612
  1.4 30.3 %collective-permute-start = (bf16[66,8,768]{2,1,0:T(8,128)(2,1)S(1)}, bf16[66,8,768]{2,1,0:T(8,128)(2,1)S(1)}, u32[]{:S(2)}, u32[]{:S(2)}) collective-permute-start(bf16[66,8,768]{2,1,0:T(8,128)(2,1)S(1)} %cut.1.own), channel_id=1, source_target_pairs={{0,8},{4,12},{8,0},{12,4},{1,9},{5,13},{9,1},{13,5},{2,10},{6,14},... | collective-permute-start | bytes 2433032 | tf_op jit(solution)/shard_map/ppermute | solution.py:29
  16.9 25.5 %collective-permute-start.3 = (bf16[67,8,768]{2,1,0:T(8,128)(2,1)S(1)}, bf16[67,8,768]{2,1,0:T(8,128)(2,1)S(1)}, u32[]{:S(2)}, u32[]{:S(2)}) collective-permute-start(bf16[67,8,768]{2,1,0:T(8,128)(2,1)S(1)} %get-tuple-element.41), channel_id=1, source_target_pairs={{0,4},{4,0},{8,12},{12,8},{1,5},{5,1},{9,13},{13,9},{2,6},{6,2},{1... | collective-permute-start | bytes 2469896 | tf_op jit(solution)/shard_map/ppermute | solution.py:29
  18.8 34.8 %collective-permute-start.5 = (bf16[67,8,768]{2,1,0:T(8,128)(2,1)S(1)}, bf16[67,8,768]{2,1,0:T(8,128)(2,1)S(1)}, u32[]{:S(2)}, u32[]{:S(2)}) collective-permute-start(bf16[67,8,768]{2,1,0:T(8,128)(2,1)S(1)} %get-tuple-element.41), channel_id=1, source_target_pairs={{0,12},{4,8},{8,4},{12,0},{1,13},{5,9},{9,5},{13,1},{2,14},{6,10},... | collective-permute-start | bytes 2469896 | tf_op jit(solution)/shard_map/ppermute | solution.py:29
  21.3 30.5 %collective-permute-start.2 = (bf16[75,8,256]{2,1,0:T(8,128)(2,1)S(1)}, bf16[75,8,256]{2,1,0:T(8,128)(2,1)S(1)}, u32[]{:S(2)}, u32[]{:S(2)}) collective-permute-start(bf16[75,8,256]{2,1,0:T(8,128)(2,1)S(1)} %get-tuple-element.33.refs_0_), channel_id=1, source_target_pairs={{0,8},{4,12},{8,0},{12,4},{1,9},{5,13},{9,1},{13,5},{2,10},{6,14},... | collective-permute-start | bytes 921608 | tf_op jit(solution)/shard_map/ppermute | solution.py:29
  31.7 25.8 %collective-permute-start.1 = (bf16[66,8,256]{2,1,0:T(8,128)(2,1)S(1)}, bf16[66,8,256]{2,1,0:T(8,128)(2,1)S(1)}, u32[]{:S(2)}, u32[]{:S(2)}) collective-permute-start(bf16[66,8,256]{2,1,0:T(8,128)(2,1)S(1)} %get-tuple-element.39), channel_id=1, source_target_pairs={{0,4},{4,0},{8,12},{12,8},{1,5},{5,1},{9,13},{13,9},{2,6},{6,2},{1... | collective-permute-start | bytes 811016 | tf_op jit(solution)/shard_map/ppermute | solution.py:29
  33.6 23.9 %collective-permute-start.4 = (bf16[66,8,256]{2,1,0:T(8,128)(2,1)S(1)}, bf16[66,8,256]{2,1,0:T(8,128)(2,1)S(1)}, u32[]{:S(2)}, u32[]{:S(2)}) collective-permute-start(bf16[66,8,256]{2,1,0:T(8,128)(2,1)S(1)} %get-tuple-element.39), channel_id=1, source_target_pairs={{0,12},{4,8},{8,4},{12,0},{1,13},{5,9},{9,5},{13,1},{2,14},{6,10},... | collective-permute-start | bytes 811016 | tf_op jit(solution)/shard_map/ppermute | solution.py:29

commit v4 on v2

--- a/solution.py
+++ b/solution.py
@@ -16,11 +16,11 @@
 BULK = 256
 TAPS = 8
 LANES = 128
-BLOCK = 256
+BLOCK = 384
 OUT_ROWS = 256
-FAR_PARTS = (768, 256)
-NEAR_PARTS = (768, 256)
-DATA_TILES = 8
+FAR_PARTS = (640, 384)
+NEAR_PARTS = (384, 384, 256)
+DATA_TILES = 6
 PIECES = 4
 TERMS = 3
 
@@ -58,12 +58,13 @@
     tail[1] = jnp.concatenate(rows).astype(jnp.bfloat16)
 
 
-def decode(data):
+def decode(data, lanes):
     if data.shape[0] == 2:
         return data[0].astype(jnp.float32), data[1].astype(jnp.float32)
     at, each = 2 * SPAN + 1, DATA_TILES // 2
     return [
-        jnp.concatenate([data[at + i * each + k].astype(jnp.float32) for k in range(each)], axis=1) for i in range(2)
+        jnp.concatenate([data[at + i * each + k].astype(jnp.float32) for k in range(each)], axis=1)[:, :lanes]
+        for i in range(2)
     ]
 
 
@@ -116,7 +117,8 @@
     width, each = far.shape[-1], DATA_TILES // 2
     for i in range(2):
         for k in range(each):
-            far[2 * SPAN + 1 + i * each + k] = near_data[i, :, k * width : (k + 1) * width]
+            some = near_data[i, :, k * width : (k + 1) * width]
+            far[2 * SPAN + 1 + i * each + k, :, 0 : some.shape[-1]] = some
 
     def add(i, total):
         block = image[:, pl.ds(i * 4, 4)].astype(jnp.float32)
@@ -222,7 +224,7 @@
 
 def table_kernel(data, table, turn, columns):
     beams = columns.shape[0]
-    taps, rest = decode(data)
+    taps, rest = decode(data, 2 * beams)
     starts = jnp.concatenate([rest[:1, :beams], rest[:1, beams:], jnp.zeros((TILE - 2, beams), jnp.float32)])
     fill = jnp.zeros((LANES - 2 * TAPS - TILE, beams), jnp.float32)
     columns[...] = jnp.transpose(jnp.concatenate([taps[:, :beams], taps[:, beams:], starts, fill]))
@@ -330,14 +332,25 @@
     )(*images, *tables, *turns, energy, *tails)
 
 
-def finish_kernel(at, skip, *refs):
-    images, tables, turns, gains = refs[0:4], refs[4:7], refs[7:10], refs[10]
-    result, buffer, sems = refs[12:15]
+def finish_kernel(at, split, *refs):
+    own, one, two, three = refs[0:split], refs[split], refs[split + 1 : 2 * split + 1], refs[2 * split + 1]
+    refs = refs[2 * split + 2 :]
+    tables, turns, gains = refs[0:3], refs[3:6], refs[6]
+    result, buffer, sems = refs[8:11]
     width = buffer.shape[-1]
     bins = slice(at, at + width)
-    own, one, two, three = images
-    cut = [own[:, :, skip : skip + width], one[...], two[:, :, skip : skip + width], three[...]]
-    both = first_merges(cut, tables, [turn[:, bins] for turn in turns], gains[...])
+
+    def piece(parts):
+        cuts, start = [], 0 if split == len(FAR_PARTS) else FAR_PARTS[0]
+        for part in parts:
+            size = part.shape[-1]
+            low, high = max(at - start, 0), min(at + width - start, size)
+            cuts.append(part[0 : 2 * SPAN, :, low:high])
+            start += size
+        return jnp.concatenate(cuts, axis=-1)
+
+    images = [piece(own), one, piece(two), three]
+    both = first_merges(images, tables, [turn[:, bins] for turn in turns], gains[...])
     copies = []
     for k, row in enumerate(range(0, buffer.shape[1], OUT_ROWS)):
         rows = slice(row, row + OUT_ROWS)
@@ -351,11 +364,12 @@
 
 
 def finish(prior, at, images, tables, turns, gains):
-    width = images[1].shape[-1]
+    own, one, two, three = images
+    width = one.shape[-1]
     beams = prior.shape[2]
-    operands = [*images, *tables, *turns, gains]
+    operands = [*own, one, *two, three, *tables, *turns, gains]
     return pl.pallas_call(
-        functools.partial(finish_kernel, at, at % FAR_PARTS[0]),
+        functools.partial(finish_kernel, at, len(own)),
         out_shape=jax.ShapeDtypeStruct(prior.shape, prior.dtype),
         in_specs=[pl.BlockSpec(memory_space=pltpu.VMEM)] * len(operands) + [pl.BlockSpec(memory_space=pl.ANY)],
         out_specs=pl.BlockSpec(memory_space=pl.ANY),
@@ -382,14 +396,20 @@
     near_table, near_turn = make_table(BAND, near_data, beams)
     last_table, last_turn = make_table(beams, last_data, beams)
     near[1], far[0], near_table, last_table = lax.optimization_barrier((near[1], far[0], near_table, last_table))
+    far_table, far_turn = make_table(BAND, far[1], beams)
+    near[2], far_table = lax.optimization_barrier((near[2], far_table))
     one, three = ([partner(part, flip) for part in near] for flip in (1, 3))
-    far_table, far_turn = make_table(BAND, far[1], beams)
 
     tables = [near_table, far_table, last_table]
     turns = [near_turn, far_turn, last_turn]
     images = [first, one[0], far[0], three[0]]
     merged, gains = merge_first(images, tables, turns, energy, [one[0], far[1], three[0]], cells, polar.shape)
-    return finish(merged, NEAR_PARTS[0], [second, one[1], far[1], three[1]], tables, turns, gains)
+    at = NEAR_PARTS[0]
+    for i in (1, 2):
+        k = int(at >= FAR_PARTS[0])
+        merged = finish(merged, at, [(first, second)[k:], one[i], far[k:], three[i]], tables, turns, gains)
+        at += NEAR_PARTS[i]
+    return merged
 
 
 def solution(mesh):

time: 58.8 us -> 58.1 us (0.988)
  the two profiles are of different devices: /device:TPU:4 before, /device:TPU:1 now
where the time goes in v4:
time: 58.1 us; the launch traced here: 57.7 us
  starting transfers between devices  26.2 us (45%)
  Pallas kernels  17.3 us (30%)
  blocking collectives  8.31 us (14%)
  waiting for transfers between devices  5.45 us (9%)
    ppermute x8, starting transfers between devices, partner(): return lax.ppermute(value, 'x', [(i, i ^ flip) for i in range(GROUP)])  26.2 us
    psum x1, blocking collectives, shards(): energy = lax.psum(energy, 'sec')  8.31 us
    pallas_call x3, Pallas kernels, make_table(): pl.pallas_call(table_kernel, out_shape=[jax.ShapeDtypeStruct(s, jnp.float...  6.6 us
    ppermute x8, waiting for transfers between devices, partner(): return lax.ppermute(value, 'x', [(i, i ^ flip) for i in range(GROUP)])  5.45 us
    pallas_call x2, Pallas kernels, finish(): pl.pallas_call(functools.partial(finish_kernel, at, len(own)), out_shape=...  4.8 us
    pallas_call x1, Pallas kernels, merge_first(): pl.pallas_call(functools.partial(merge_kernel, cells), grid=(width // BLO...  2.8 us
    pallas_call x1, Pallas kernels, prepare(): pl.pallas_call(prepare_kernel, grid=(1,), out_shape=shapes, in_specs=[*se...  1.75 us
    pallas_call x1, Pallas kernels, cut(): pl.pallas_call(cut_kernel, out_shape=jax.ShapeDtypeStruct((2 * SPAN, TILE...  1.29 us
  transfers between devices with their start and end apart: 8, of which 4 were waited for; matrix products, arithmetic and copies ran while one was open for 0% of the time, Pallas kernels for 24%

profile of v4, /device:TPU:1, one launch (start us, length us, event | category | flops | bytes accessed | tf_op | source)
XLA Modules:
  0.0 57.7 jit_solution(439587391876757506)
XLA Ops:
  0.0 0.0 copy-start.1
  0.0 0.0 copy-start.2
  0.0 0.0 copy-start
  0.0 1.3 %cut.1.refs_0_ = bf16[66,8,640]{2,1,0:T(8,128)(2,1)S(1)} custom-call(bf16[2,64,8,1024]{3,2,1,0:T(8,128)(2,1)} %bitcast.1), custom_call_target="tpu_custom_call" | custom-call | bytes 1600000 | tf_op jit(solution)/shard_map/cut/pallas_call | solution.py:86
  1.3 5.5 %collective-permute-start.3 = (bf16[66,8,640]{2,1,0:T(8,128)(2,1)S(1)}, bf16[66,8,640]{2,1,0:T(8,128)(2,1)S(1)}, u32[]{:S(2)}, u32[]{:S(2)}) collective-permute-start(bf16[66,8,640]{2,1,0:T(8,128)(2,1)S(1)} %cut.1.refs_0_), channel_id=1, source_target_pairs={{0,8},{4,12},{8,0},{12,4},{1,9},{5,13},{9,1},{13,5},{2,10},{6,14},... | collective-permute-start | bytes 2027528 | tf_op jit(solution)/shard_map/ppermute | solution.py:29
  6.8 0.0 copy-done.1
  6.8 0.0 copy-done.2
  6.8 0.0 copy-done
  6.8 1.7 %prepare.1 = (bf16[73,8,384]{2,1,0:T(8,128)(2,1)S(1)}, bf16[67,8,384]{2,1,0:T(8,128)(2,1)S(1)}, bf16[66,8,384]{2,1,0:T(8,128)(2,1)S(1)}, bf16[66,8,256]{2,1,0:T(...) custom-call(f32[2,2,1,8,512]{4,3,2,1,0:T(8,128)S(1)} %copy-done, ...), custom_call_target="tpu_custom_call" | custom-call | flops 1081344 | bytes 4000000 | tf_op jit(solution)/shard_map/prepare/pallas_call | solution.py:148
  8.6 8.3 %psum.7.energy.refs_10_ = f32[1,128]{1,0:T(1,128)S(1)} all-reduce(f32[1,128]{1,0:T(1,128)S(1)} %get-tuple-element.33), channel_id=1, replica_groups=mesh['rest'=32,'x'=4,'sec'=4] {'sec'}, use_global_device_ids=true, to_apply=%region_0.0 | all-reduce | flops 128 | bytes 1024 | tf_op jit(solution)/shard_map/psum | solution.py:393
  16.9 5.1 %collective-permute-start = (bf16[73,8,384]{2,1,0:T(8,128)(2,1)S(1)}, bf16[73,8,384]{2,1,0:T(8,128)(2,1)S(1)}, u32[]{:S(2)}, u32[]{:S(2)}) collective-permute-start(bf16[73,8,384]{2,1,0:T(8,128)(2,1)S(1)} %get-tuple-element.34.refs_1_.refs_0_), channel_id=1, source_target_pairs={{0,8},{4,12},{8,0},{12,4},{1,9},{5,13},{9,1},{13,5},{2,10},{6,14},... | collective-permute-start | bytes 1345544 | tf_op jit(solution)/shard_map/ppermute | solution.py:29
  22.1 1.9 %collective-permute-start.4 = (bf16[67,8,384]{2,1,0:T(8,128)(2,1)S(1)}, bf16[67,8,384]{2,1,0:T(8,128)(2,1)S(1)}, u32[]{:S(2)}, u32[]{:S(2)}) collective-permute-start(bf16[67,8,384]{2,1,0:T(8,128)(2,1)S(1)} %get-tuple-element.50), channel_id=1, source_target_pairs={{0,4},{4,0},{8,12},{12,8},{1,5},{5,1},{9,13},{13,9},{2,6},{6,2},{1... | collective-permute-start | bytes 1234952 | tf_op jit(solution)/shard_map/ppermute | solution.py:29
  24.0 2.2 %collective-permute-start.5 = (bf16[67,8,384]{2,1,0:T(8,128)(2,1)S(1)}, bf16[67,8,384]{2,1,0:T(8,128)(2,1)S(1)}, u32[]{:S(2)}, u32[]{:S(2)}) collective-permute-start(bf16[67,8,384]{2,1,0:T(8,128)(2,1)S(1)} %get-tuple-element.50), channel_id=1, source_target_pairs={{0,12},{4,8},{8,4},{12,0},{1,13},{5,9},{9,5},{13,1},{2,14},{6,10},... | collective-permute-start | bytes 1234952 | tf_op jit(solution)/shard_map/ppermute | solution.py:29
  26.2 2.9 %table.5 = (f32[512,528]{1,0:T(8,128)S(1)}, f32[4,1024]{1,0:T(4,128)S(1)}) custom-call(bf16[2,8,1024]{2,1,0:T(8,128)(2,1)S(1)} %get-tuple-element.41.data), custom_call_target="tpu_custom_call" | custom-call | flops 6144000 | bytes 2097152 | tf_op jit(solution)/shard_map/table/pallas_call | solution.py:243
  29.1 0.1 convert_element_type.11.refs_6_.refs_8_
  29.2 1.8 %table.4 = (f32[264,528]{1,0:T(8,128)S(1)}, f32[4,1024]{1,0:T(4,128)S(1)}) custom-call(bf16[2,8,1024]{2,1,0:T(8,128)(2,1)S(1)} %get-tuple-element.39.data), custom_call_target="tpu_custom_call" | custom-call | flops 3168000 | bytes 1081344 | tf_op jit(solution)/shard_map/table/pallas_call | solution.py:243
  31.1 0.0 collective-permute-done.3.refs_2_.refs_3_
  31.1 3.1 %collective-permute-start.6 = (bf16[66,8,384]{2,1,0:T(8,128)(2,1)S(1)}, bf16[66,8,384]{2,1,0:T(8,128)(2,1)S(1)}, u32[]{:S(2)}, u32[]{:S(2)}) collective-permute-start(bf16[66,8,384]{2,1,0:T(8,128)(2,1)S(1)} %get-tuple-element.53), channel_id=1, source_target_pairs={{0,4},{4,0},{8,12},{12,8},{1,5},{5,1},{9,13},{13,9},{2,6},{6,2},{1... | collective-permute-start | bytes 1216520 | tf_op jit(solution)/shard_map/ppermute | solution.py:29
  34.2 4.0 %collective-permute-start.7 = (bf16[66,8,384]{2,1,0:T(8,128)(2,1)S(1)}, bf16[66,8,384]{2,1,0:T(8,128)(2,1)S(1)}, u32[]{:S(2)}, u32[]{:S(2)}) collective-permute-start(bf16[66,8,384]{2,1,0:T(8,128)(2,1)S(1)} %get-tuple-element.53), channel_id=1, source_target_pairs={{0,12},{4,8},{8,4},{12,0},{1,13},{5,9},{9,5},{13,1},{2,14},{6,10},... | collective-permute-start | bytes 1216520 | tf_op jit(solution)/shard_map/ppermute | solution.py:29
  38.2 0.0 collective-permute-done.data.refs_12_.refs_4_.refs_2_
  38.2 1.9 %table.3 = (f32[264,528]{1,0:T(8,128)S(1)}, f32[4,1024]{1,0:T(4,128)S(1)}) custom-call(bf16[73,8,384]{2,1,0:T(8,128)(2,1)S(1)} %collective-permute-done.data.refs_12_.refs_4_.refs_2_), custom_call_target="tpu_custom_call" | custom-call | flops 3168000 | bytes 1081344 | tf_op jit(solution)/shard_map/table/pallas_call | solution.py:243
  40.1 1.9 %collective-permute-start.1 = (bf16[66,8,256]{2,1,0:T(8,128)(2,1)S(1)}, bf16[66,8,256]{2,1,0:T(8,128)(2,1)S(1)}, u32[]{:S(2)}, u32[]{:S(2)}) collective-permute-start(bf16[66,8,256]{2,1,0:T(8,128)(2,1)S(1)} %get-tuple-element.37), channel_id=1, source_target_pairs={{0,4},{4,0},{8,12},{12,8},{1,5},{5,1},{9,13},{13,9},{2,6},{6,2},{1... | collective-permute-start | bytes 811016 | tf_op jit(solution)/shard_map/ppermute | solution.py:29
  42.0 0.0 collective-permute-done.4.refs_1_.refs_11_
  42.1 2.5 %collective-permute-start.2 = (bf16[66,8,256]{2,1,0:T(8,128)(2,1)S(1)}, bf16[66,8,256]{2,1,0:T(8,128)(2,1)S(1)}, u32[]{:S(2)}, u32[]{:S(2)}) collective-permute-start(bf16[66,8,256]{2,1,0:T(8,128)(2,1)S(1)} %get-tuple-element.37), channel_id=1, source_target_pairs={{0,12},{4,8},{8,4},{12,0},{1,13},{5,9},{9,5},{13,1},{2,14},{6,10},... | collective-permute-start | bytes 811016 | tf_op jit(solution)/shard_map/ppermute | solution.py:29
  44.6 0.0 collective-permute-done.5.refs_3_.refs_13_
  44.6 2.8 %merge.1 = (bf16[1,2,512,1024]{3,2,1,0:T(8,128)(2,1)}, f32[4,128]{1,0:T(4,128)S(1)}) custom-call(bf16[66,8,640]{2,1,0:T(8,128)(2,1)S(1)} %cut.1.refs_0_, bf16[67,8,384]{2,1,0:T(8,128)(2,1)S(1)} %collective-permute-done.4.refs_1_.refs_11_, bf16[66,8,640]{2,1,0:T(8,128)(2,1)S(1)} %collective-permute-done.3.refs_2_.refs_3_, ...), custom_call_target="tpu_custom_call" | custom-call | flops 843448320 | bytes 3145728 | tf_op jit(solution)/shard_map/merge/pallas_call | solution.py:320
  47.4 1.4 %collective-permute-done.6.refs_2_ = bf16[66,8,384]{2,1,0:T(8,128)(2,1)S(1)} collective-permute-done((bf16[66,8,384]{2,1,0:T(8,128)(2,1)S(1)}, bf16[66,8,384]{2,1,0:T(8,128)(2,1)S(1)}, u32[]{:S(2)}, u32[]{:S(2)}) %collective-permute-start.6) | collective-permute-done | bytes 405536 | tf_op jit(solution)/shard_map/ppermute | solution.py:29
  48.8 1.0 %collective-permute-done.7.refs_5_ = bf16[66,8,384]{2,1,0:T(8,128)(2,1)S(1)} collective-permute-done((bf16[66,8,384]{2,1,0:T(8,128)(2,1)S(1)}, bf16[66,8,384]{2,1,0:T(8,128)(2,1)S(1)}, u32[]{:S(2)}, u32[]{:S(2)}) %collective-permute-start.7) | collective-permute-done | bytes 405536 | tf_op jit(solution)/shard_map/ppermute | solution.py:29
  49.9 2.8 %finish.2.refs_11_ = bf16[1,2,512,1024]{3,2,1,0:T(8,128)(2,1)} custom-call(bf16[66,8,640]{2,1,0:T(8,128)(2,1)S(1)} %cut.1.refs_0_, bf16[73,8,384]{2,1,0:T(8,128)(2,1)S(1)} %get-tuple-element.34.refs_1_.refs_0_, bf16[66,8,384]{2,1,0:T(8,128)(2,1)S(1)} %collective-permute-done.6.refs_2_, ...), custom_call_target="tpu_custom_call", output_to_operand_aliasing={{}: (13, {})} | custom-call | flops 843448320 | bytes 3145728 | tf_op jit(solution)/shard_map/finish/pallas_call | solution.py:371
  52.7 1.9 %collective-permute-done.1.refs_1_ = bf16[66,8,256]{2,1,0:T(8,128)(2,1)S(1)} collective-permute-done((bf16[66,8,256]{2,1,0:T(8,128)(2,1)S(1)}, bf16[66,8,256]{2,1,0:T(8,128)(2,1)S(1)}, u32[]{:S(2)}, u32[]{:S(2)}) %collective-permute-start.1) | collective-permute-done | bytes 270368 | tf_op jit(solution)/shard_map/ppermute | solution.py:29
  54.6 1.0 %collective-permute-done.2.refs_3_ = bf16[66,8,256]{2,1,0:T(8,128)(2,1)S(1)} collective-permute-done((bf16[66,8,256]{2,1,0:T(8,128)(2,1)S(1)}, bf16[66,8,256]{2,1,0:T(8,128)(2,1)S(1)}, u32[]{:S(2)}, u32[]{:S(2)}) %collective-permute-start.2) | collective-permute-done | bytes 270368 | tf_op jit(solution)/shard_map/ppermute | solution.py:29
  55.7 2.0 %finish.3 = bf16[1,2,512,1024]{3,2,1,0:T(8,128)(2,1)} custom-call(bf16[73,8,384]{2,1,0:T(8,128)(2,1)S(1)} %get-tuple-element.34.refs_1_.refs_0_, bf16[66,8,256]{2,1,0:T(8,128)(2,1)S(1)} %collective-permute-done.1.refs_1_, bf16[73,8,384]{2,1,0:T(8,128)(2,1)S(1)} %collective-permute-done.data.refs_12_.refs_4_.refs_2_, ...), custom_call_target="tpu_custom_call", output_to_operand_aliasing={{}: (11, {})} | custom-call | flops 562298880 | bytes 2097152 | tf_op jit(solution)/shard_map/finish/pallas_call | solution.py:371
  (3 shorter events, 0.1 us)
Async XLA Ops:
  0.0 6.8 %copy-start.1 = (f32[2,2,1,1024]{3,2,1,0:T(1,128)S(1)}, f32[2,2,1,1024]{3,2,1,0:T(1,128)}, u32[]{:S(2)}) copy-start(f32[2,2,1,1024]{3,2,1,0:T(1,128)} %refs_5_.1) | copy-start | bytes 49156
  0.0 6.8 %copy-start.2 = (s32[2,2,1,512]{3,2,1,0:T(1,128)S(1)}, s32[2,2,1,512]{3,2,1,0:T(1,128)}, u32[]{:S(2)}) copy-start(s32[2,2,1,512]{3,2,1,0:T(1,128)} %refs_4_.1) | copy-start | bytes 24580
  0.0 6.8 %copy-start = (f32[2,2,1,8,512]{4,3,2,1,0:T(8,128)S(1)}, f32[2,2,1,8,512]{4,3,2,1,0:T(8,128)}, u32[]{:S(2)}) copy-start(f32[2,2,1,8,512]{4,3,2,1,0:T(8,128)} %refs_3_.1) | copy-start | bytes 196612
  1.3 29.8 %collective-permute-start.3 = (bf16[66,8,640]{2,1,0:T(8,128)(2,1)S(1)}, bf16[66,8,640]{2,1,0:T(8,128)(2,1)S(1)}, u32[]{:S(2)}, u32[]{:S(2)}) collective-permute-start(bf16[66,8,640]{2,1,0:T(8,128)(2,1)S(1)} %cut.1.refs_0_), channel_id=1, source_target_pairs={{0,8},{4,12},{8,0},{12,4},{1,9},{5,13},{9,1},{13,5},{2,10},{6,14},... | collective-permute-start | bytes 2027528 | tf_op jit(solution)/shard_map/ppermute | solution.py:29
  16.9 21.3 %collective-permute-start = (bf16[73,8,384]{2,1,0:T(8,128)(2,1)S(1)}, bf16[73,8,384]{2,1,0:T(8,128)(2,1)S(1)}, u32[]{:S(2)}, u32[]{:S(2)}) collective-permute-start(bf16[73,8,384]{2,1,0:T(8,128)(2,1)S(1)} %get-tuple-element.34.refs_1_.refs_0_), channel_id=1, source_target_pairs={{0,8},{4,12},{8,0},{12,4},{1,9},{5,13},{9,1},{13,5},{2,10},{6,14},... | collective-permute-start | bytes 1345544 | tf_op jit(solution)/shard_map/ppermute | solution.py:29
  22.1 20.0 %collective-permute-start.4 = (bf16[67,8,384]{2,1,0:T(8,128)(2,1)S(1)}, bf16[67,8,384]{2,1,0:T(8,128)(2,1)S(1)}, u32[]{:S(2)}, u32[]{:S(2)}) collective-permute-start(bf16[67,8,384]{2,1,0:T(8,128)(2,1)S(1)} %get-tuple-element.50), channel_id=1, source_target_pairs={{0,4},{4,0},{8,12},{12,8},{1,5},{5,1},{9,13},{13,9},{2,6},{6,2},{1... | collective-permute-start | bytes 1234952 | tf_op jit(solution)/shard_map/ppermute | solution.py:29
  24.0 20.6 %collective-permute-start.5 = (bf16[67,8,384]{2,1,0:T(8,128)(2,1)S(1)}, bf16[67,8,384]{2,1,0:T(8,128)(2,1)S(1)}, u32[]{:S(2)}, u32[]{:S(2)}) collective-permute-start(bf16[67,8,384]{2,1,0:T(8,128)(2,1)S(1)} %get-tuple-element.50), channel_id=1, source_target_pairs={{0,12},{4,8},{8,4},{12,0},{1,13},{5,9},{9,5},{13,1},{2,14},{6,10},... | collective-permute-start | bytes 1234952 | tf_op jit(solution)/shard_map/ppermute | solution.py:29
  31.1 17.7 %collective-permute-start.6 = (bf16[66,8,384]{2,1,0:T(8,128)(2,1)S(1)}, bf16[66,8,384]{2,1,0:T(8,128)(2,1)S(1)}, u32[]{:S(2)}, u32[]{:S(2)}) collective-permute-start(bf16[66,8,384]{2,1,0:T(8,128)(2,1)S(1)} %get-tuple-element.53), channel_id=1, source_target_pairs={{0,4},{4,0},{8,12},{12,8},{1,5},{5,1},{9,13},{13,9},{2,6},{6,2},{1... | collective-permute-start | bytes 1216520 | tf_op jit(solution)/shard_map/ppermute | solution.py:29
  34.2 15.6 %collective-permute-start.7 = (bf16[66,8,384]{2,1,0:T(8,128)(2,1)S(1)}, bf16[66,8,384]{2,1,0:T(8,128)(2,1)S(1)}, u32[]{:S(2)}, u32[]{:S(2)}) collective-permute-start(bf16[66,8,384]{2,1,0:T(8,128)(2,1)S(1)} %get-tuple-element.53), channel_id=1, source_target_pairs={{0,12},{4,8},{8,4},{12,0},{1,13},{5,9},{9,5},{13,1},{2,14},{6,10},... | collective-permute-start | bytes 1216520 | tf_op jit(solution)/shard_map/ppermute | solution.py:29
  40.1 14.5 %collective-permute-start.1 = (bf16[66,8,256]{2,1,0:T(8,128)(2,1)S(1)}, bf16[66,8,256]{2,1,0:T(8,128)(2,1)S(1)}, u32[]{:S(2)}, u32[]{:S(2)}) collective-permute-start(bf16[66,8,256]{2,1,0:T(8,128)(2,1)S(1)} %get-tuple-element.37), channel_id=1, source_target_pairs={{0,4},{4,0},{8,12},{12,8},{1,5},{5,1},{9,13},{13,9},{2,6},{6,2},{1... | collective-permute-start | bytes 811016 | tf_op jit(solution)/shard_map/ppermute | solution.py:29
  42.1 13.6 %collective-permute-start.2 = (bf16[66,8,256]{2,1,0:T(8,128)(2,1)S(1)}, bf16[66,8,256]{2,1,0:T(8,128)(2,1)S(1)}, u32[]{:S(2)}, u32[]{:S(2)}) collective-permute-start(bf16[66,8,256]{2,1,0:T(8,128)(2,1)S(1)} %get-tuple-element.37), channel_id=1, source_target_pairs={{0,12},{4,8},{8,4},{12,0},{1,13},{5,9},{9,5},{13,1},{2,14},{6,10},... | collective-permute-start | bytes 811016 | tf_op jit(solution)/shard_map/ppermute | solution.py:29

commit v5 on v4

--- a/solution.py
+++ b/solution.py
@@ -264,19 +264,21 @@
     return jnp.concatenate(both, axis=1)
 
 
+def child(source, turn, row, gain):
+    width = source.shape[-1]
+    real, imag = (source[half * SPAN : (half + 1) * SPAN].astype(jnp.float32).reshape(BAND, width) for half in range(2))
+    scale = jnp.concatenate([gain] * (width // LANES), axis=1)
+    return turned(real, imag, scale * turn[row : row + 1, :], scale * turn[row + 1 : row + 2, :])
+
+
+def halves(merged):
+    width = merged.shape[1] // 2
+    return merged[:, :width], merged[:, width:]
+
+
 def first_merges(images, tables, turns, gains):
-    width = images[1].shape[-1]
-
-    def child(source, turn, row, gain):
-        real, imag = (
-            source[half * SPAN : (half + 1) * SPAN].astype(jnp.float32).reshape(BAND, width) for half in range(2)
-        )
-        scale = jnp.concatenate([gain] * (width // LANES), axis=1)
-        return turned(real, imag, scale * turn[row : row + 1, :], scale * turn[row + 1 : row + 2, :])
-
     def merge(left, right, table):
-        merged = jnp.dot(table[...], joined(left, right), preferred_element_type=jnp.float32)
-        return merged[:, :width], merged[:, width:]
+        return halves(jnp.dot(table[...], joined(left, right), preferred_element_type=jnp.float32))
 
     own, one, two, three = images
     near_turn, far_turn, last_turn = turns
@@ -285,6 +287,63 @@
     far = merge(child(two, far_turn, 0, gains[2:3]), child(three, far_turn, 2, gains[3:4]), tables[1])
     far = turned(*far, last_turn[2:3, :], last_turn[3:4, :])
     return joined(near, far)
+
+
+def ready_kernel(at, own, two, near_table, far_table, near_turn, far_turn, gains, result):
+    width = result.shape[-1] // 2
+    skip = at - FAR_PARTS[0]
+    bins = slice(at, at + width)
+    pairs = ((own, near_table, near_turn, 0), (two, far_table, far_turn, 2))
+    for i, (source, table, turn, k) in enumerate(pairs):
+        source = source[0 : 2 * SPAN, :, skip : skip + width]
+        rows = jnp.concatenate(child(source, turn[:, bins], 0, gains[k : k + 1, :]), axis=1)
+        rest = jnp.concatenate([rows[BULK:], jnp.zeros((TILE, 2 * width), jnp.float32)])
+        bulk = jnp.dot(table[:, 0:BULK], rows[:BULK].astype(jnp.bfloat16), preferred_element_type=jnp.float32)
+        tail = jnp.dot(table[:, 2 * BULK :], rest.astype(jnp.bfloat16), preferred_element_type=jnp.float32)
+        result[i] = bulk + tail
+
+
+def ready(at, width, own, two, tables, turns, gains):
+    operands = [own, two, *tables, *turns, gains]
+    return pl.pallas_call(
+        functools.partial(ready_kernel, at),
+        out_shape=jax.ShapeDtypeStruct((2, BAND, 2 * width), jnp.float32),
+        in_specs=[pl.BlockSpec(memory_space=pltpu.VMEM)] * len(operands),
+        out_specs=pl.BlockSpec(memory_space=pltpu.VMEM),
+        compiler_params=pltpu.CompilerParams(vmem_limit_bytes=12 * 2**20),
+        cost_estimate=merge_cost(width, BAND),
+        name="ready",
+    )(*operands)
+
+
+def last_kernel(at, *refs):
+    made, one, three, near_table, far_table, last_table, near_turn, far_turn, last_turn, gains = refs[:10]
+    result, buffer, sems = refs[11:14]
+    width = buffer.shape[-1]
+    bins = slice(at, at + width)
+
+    def merge(i, source, table, turn, k):
+        rows = jnp.concatenate(child(source, turn[:, bins], 2, gains[k : k + 1, :]), axis=1)
+        rows = jnp.concatenate([rows[:BULK], jnp.zeros((TILE, 2 * width), jnp.float32), rows[BULK:]])
+        added = jnp.dot(table[:, BULK:], rows.astype(jnp.bfloat16), preferred_element_type=jnp.float32)
+        turns = last_turn[2 * i : 2 * i + 2, bins]
+        return turned(*halves(made[i] + added), turns[0:1], turns[1:2])
+
+    both = joined(merge(0, one, near_table, near_turn, 1), merge(1, three, far_table, far_turn, 3))
+    write_out(both, last_table, buffer, result, bins, sems)
+
+
+def write_out(both, table, buffer, result, bins, sems):
+    copies = []
+    for k, row in enumerate(range(0, buffer.shape[1], OUT_ROWS)):
+        rows = slice(row, row + OUT_ROWS)
+        merged = jnp.dot(table[rows, :], both, preferred_element_type=jnp.float32)
+        for half, part in enumerate(halves(merged)):
+            buffer[half, rows] = part.astype(jnp.bfloat16)
+        copies.append(pltpu.make_async_copy(buffer.at[:, rows], result.at[0, :, rows, bins], sems.at[k]))
+        copies[-1].start()
+    for copy in copies:
+        copy.wait()
 
 
 def merge_kernel(cells, *refs):
@@ -351,25 +410,13 @@
 
     images = [piece(own), one, piece(two), three]
     both = first_merges(images, tables, [turn[:, bins] for turn in turns], gains[...])
-    copies = []
-    for k, row in enumerate(range(0, buffer.shape[1], OUT_ROWS)):
-        rows = slice(row, row + OUT_ROWS)
-        merged = jnp.dot(tables[2][rows, :], both, preferred_element_type=jnp.float32)
-        for half in range(2):
-            buffer[half, rows] = merged[:, half * width : (half + 1) * width].astype(jnp.bfloat16)
-        copies.append(pltpu.make_async_copy(buffer.at[:, rows], result.at[0, :, rows, bins], sems.at[k]))
-        copies[-1].start()
-    for copy in copies:
-        copy.wait()
-
-
-def finish(prior, at, images, tables, turns, gains):
-    own, one, two, three = images
-    width = one.shape[-1]
+    write_out(both, tables[2], buffer, result, bins, sems)
+
+
+def finish(kernel, prior, width, operands):
     beams = prior.shape[2]
-    operands = [*own, one, *two, three, *tables, *turns, gains]
-    return pl.pallas_call(
-        functools.partial(finish_kernel, at, len(own)),
+    return pl.pallas_call(
+        kernel,
         out_shape=jax.ShapeDtypeStruct(prior.shape, prior.dtype),
         in_specs=[pl.BlockSpec(memory_space=pltpu.VMEM)] * len(operands) + [pl.BlockSpec(memory_space=pl.ANY)],
         out_specs=pl.BlockSpec(memory_space=pl.ANY),
@@ -404,12 +451,13 @@
     turns = [near_turn, far_turn, last_turn]
     images = [first, one[0], far[0], three[0]]
     merged, gains = merge_first(images, tables, turns, energy, [one[0], far[1], three[0]], cells, polar.shape)
-    at = NEAR_PARTS[0]
-    for i in (1, 2):
-        k = int(at >= FAR_PARTS[0])
-        merged = finish(merged, at, [(first, second)[k:], one[i], far[k:], three[i]], tables, turns, gains)
-        at += NEAR_PARTS[i]
-    return merged
+    at, width = NEAR_PARTS[:2]
+    operands = [first, second, one[1], *far, three[1], *tables, *turns, gains]
+    merged = finish(functools.partial(finish_kernel, at, 2), merged, width, operands)
+    at, width = at + width, NEAR_PARTS[2]
+    made = ready(at, width, second, far[1], tables[:2], turns[:2], gains)
+    operands = [made, one[2], three[2], *tables, *turns, gains]
+    return finish(functools.partial(last_kernel, at), merged, width, operands)
 
 
 def solution(mesh):

time: 58.1 us -> 57.9 us (level)
    pallas_call x2 -> x3, Pallas kernels: 4.8 us -> 5.14 us  [the longest x2 4.7 us: finish(): pl.pallas_call(kernel, out_shape=jax.ShapeDtypeStruct(prior.shape, prior....]
  transfers between devices with their start and end apart: 8 -> 8, of which waited for: 4 -> 4; matrix products, arithmetic and copies ran while one was open for 0% -> 0% of each run, Pallas kernels for 24% -> 25%
where the time goes in v5:
time: 57.9 us; the launch traced here: 57.5 us
  starting transfers between devices  26.2 us (45%)
  Pallas kernels  17.7 us (31%)
  blocking collectives  8.31 us (14%)
  waiting for transfers between devices  4.93 us (9%)
    ppermute x8, starting transfers between devices, partner(): return lax.ppermute(value, 'x', [(i, i ^ flip) for i in range(GROUP)])  26.2 us
    psum x1, blocking collectives, shards(): energy = lax.psum(energy, 'sec')  8.31 us
    pallas_call x3, Pallas kernels, make_table(): pl.pallas_call(table_kernel, out_shape=[jax.ShapeDtypeStruct(s, jnp.float...  6.6 us
    ppermute x8, waiting for transfers between devices, partner(): return lax.ppermute(value, 'x', [(i, i ^ flip) for i in range(GROUP)])  4.93 us
    pallas_call x2, Pallas kernels, finish(): pl.pallas_call(kernel, out_shape=jax.ShapeDtypeStruct(prior.shape, prior....  4.7 us
    pallas_call x1, Pallas kernels, merge_first(): pl.pallas_call(functools.partial(merge_kernel, cells), grid=(width // BLO...  2.84 us
    pallas_call x1, Pallas kernels, prepare(): pl.pallas_call(prepare_kernel, grid=(1,), out_shape=shapes, in_specs=[*se...  1.75 us
    pallas_call x1, Pallas kernels, cut(): pl.pallas_call(cut_kernel, out_shape=jax.ShapeDtypeStruct((2 * SPAN, TILE...  1.29 us
  transfers between devices with their start and end apart: 8, of which 4 were waited for; matrix products, arithmetic and copies ran while one was open for 0% of the time, Pallas kernels for 25%

profile of v5, /device:TPU:1, one launch (start us, length us, event | category | flops | bytes accessed | tf_op | source)
XLA Modules:
  0.0 57.5 jit_solution(17913360776047301571)
XLA Ops:
  0.0 0.0 copy-start.1
  0.0 0.0 copy-start.2
  0.0 1.3 %cut.1.refs_0_ = bf16[66,8,640]{2,1,0:T(8,128)(2,1)S(1)} custom-call(bf16[2,64,8,1024]{3,2,1,0:T(8,128)(2,1)} %bitcast.1), custom_call_target="tpu_custom_call" | custom-call | bytes 1600000 | tf_op jit(solution)/shard_map/cut/pallas_call | solution.py:86
  1.3 5.5 %collective-permute-start.1 = (bf16[66,8,640]{2,1,0:T(8,128)(2,1)S(1)}, bf16[66,8,640]{2,1,0:T(8,128)(2,1)S(1)}, u32[]{:S(2)}, u32[]{:S(2)}) collective-permute-start(bf16[66,8,640]{2,1,0:T(8,128)(2,1)S(1)} %cut.1.refs_0_), channel_id=1, source_target_pairs={{0,8},{4,12},{8,0},{12,4},{1,9},{5,13},{9,1},{13,5},{2,10},{6,14},... | collective-permute-start | bytes 2027528 | tf_op jit(solution)/shard_map/ppermute | solution.py:29
  6.8 0.0 copy-done.1
  6.8 0.0 copy-done.2
  6.8 0.0 copy-done
  6.8 1.7 %prepare.1 = (bf16[73,8,384]{2,1,0:T(8,128)(2,1)S(1)}, bf16[67,8,384]{2,1,0:T(8,128)(2,1)S(1)}, bf16[66,8,384]{2,1,0:T(8,128)(2,1)S(1)}, bf16[66,8,256]{2,1,0:T(...) custom-call(f32[2,2,1,8,512]{4,3,2,1,0:T(8,128)S(1)} %copy-done, ...), custom_call_target="tpu_custom_call" | custom-call | flops 1081344 | bytes 4000000 | tf_op jit(solution)/shard_map/prepare/pallas_call | solution.py:148
  8.6 8.3 %psum.7.energy.refs_10_ = f32[1,128]{1,0:T(1,128)S(1)} all-reduce(f32[1,128]{1,0:T(1,128)S(1)} %get-tuple-element.33), channel_id=1, replica_groups=mesh['rest'=32,'x'=4,'sec'=4] {'sec'}, use_global_device_ids=true, to_apply=%region_0.0 | all-reduce | flops 128 | bytes 1024 | tf_op jit(solution)/shard_map/psum | solution.py:440
  16.9 5.1 %collective-permute-start = (bf16[73,8,384]{2,1,0:T(8,128)(2,1)S(1)}, bf16[73,8,384]{2,1,0:T(8,128)(2,1)S(1)}, u32[]{:S(2)}, u32[]{:S(2)}) collective-permute-start(bf16[73,8,384]{2,1,0:T(8,128)(2,1)S(1)} %get-tuple-element.34.own.refs_1_), channel_id=1, source_target_pairs={{0,8},{4,12},{8,0},{12,4},{1,9},{5,13},{9,1},{13,5},{2,10},{6,14},... | collective-permute-start | bytes 1345544 | tf_op jit(solution)/shard_map/ppermute | solution.py:29
  22.1 1.9 %collective-permute-start.2 = (bf16[67,8,384]{2,1,0:T(8,128)(2,1)S(1)}, bf16[67,8,384]{2,1,0:T(8,128)(2,1)S(1)}, u32[]{:S(2)}, u32[]{:S(2)}) collective-permute-start(bf16[67,8,384]{2,1,0:T(8,128)(2,1)S(1)} %get-tuple-element.47), channel_id=1, source_target_pairs={{0,4},{4,0},{8,12},{12,8},{1,5},{5,1},{9,13},{13,9},{2,6},{6,2},{1... | collective-permute-start | bytes 1234952 | tf_op jit(solution)/shard_map/ppermute | solution.py:29
  24.0 2.2 %collective-permute-start.3 = (bf16[67,8,384]{2,1,0:T(8,128)(2,1)S(1)}, bf16[67,8,384]{2,1,0:T(8,128)(2,1)S(1)}, u32[]{:S(2)}, u32[]{:S(2)}) collective-permute-start(bf16[67,8,384]{2,1,0:T(8,128)(2,1)S(1)} %get-tuple-element.47), channel_id=1, source_target_pairs={{0,12},{4,8},{8,4},{12,0},{1,13},{5,9},{9,5},{13,1},{2,14},{6,10},... | collective-permute-start | bytes 1234952 | tf_op jit(solution)/shard_map/ppermute | solution.py:29
  26.2 2.9 %table.4 = (f32[512,528]{1,0:T(8,128)S(1)}, f32[4,1024]{1,0:T(4,128)S(1)}) custom-call(bf16[2,8,1024]{2,1,0:T(8,128)(2,1)S(1)} %get-tuple-element.38.data), custom_call_target="tpu_custom_call" | custom-call | flops 6144000 | bytes 2097152 | tf_op jit(solution)/shard_map/table/pallas_call | solution.py:243
  29.1 0.1 convert_element_type.10.refs_6_.refs_8_.refs_5_
  29.2 1.8 %table.3 = (f32[264,528]{1,0:T(8,128)S(1)}, f32[4,1024]{1,0:T(4,128)S(1)}) custom-call(bf16[2,8,1024]{2,1,0:T(8,128)(2,1)S(1)} %get-tuple-element.36.data), custom_call_target="tpu_custom_call" | custom-call | flops 3168000 | bytes 1081344 | tf_op jit(solution)/shard_map/table/pallas_call | solution.py:243
  31.1 0.0 collective-permute-done.1.refs_2_.refs_3_
  31.1 3.1 %collective-permute-start.6 = (bf16[66,8,384]{2,1,0:T(8,128)(2,1)S(1)}, bf16[66,8,384]{2,1,0:T(8,128)(2,1)S(1)}, u32[]{:S(2)}, u32[]{:S(2)}) collective-permute-start(bf16[66,8,384]{2,1,0:T(8,128)(2,1)S(1)} %get-tuple-element.53), channel_id=1, source_target_pairs={{0,4},{4,0},{8,12},{12,8},{1,5},{5,1},{9,13},{13,9},{2,6},{6,2},{1... | collective-permute-start | bytes 1216520 | tf_op jit(solution)/shard_map/ppermute | solution.py:29
  34.2 4.0 %collective-permute-start.7 = (bf16[66,8,384]{2,1,0:T(8,128)(2,1)S(1)}, bf16[66,8,384]{2,1,0:T(8,128)(2,1)S(1)}, u32[]{:S(2)}, u32[]{:S(2)}) collective-permute-start(bf16[66,8,384]{2,1,0:T(8,128)(2,1)S(1)} %get-tuple-element.53), channel_id=1, source_target_pairs={{0,12},{4,8},{8,4},{12,0},{1,13},{5,9},{9,5},{13,1},{2,14},{6,10},... | collective-permute-start | bytes 1216520 | tf_op jit(solution)/shard_map/ppermute | solution.py:29
  38.2 0.0 collective-permute-done.data.refs_12_.two.refs_4_
  38.2 1.9 %table.5 = (f32[264,528]{1,0:T(8,128)S(1)}, f32[4,1024]{1,0:T(4,128)S(1)}) custom-call(bf16[73,8,384]{2,1,0:T(8,128)(2,1)S(1)} %collective-permute-done.data.refs_12_.two.refs_4_), custom_call_target="tpu_custom_call" | custom-call | flops 3168000 | bytes 1081344 | tf_op jit(solution)/shard_map/table/pallas_call | solution.py:243
  40.1 1.9 %collective-permute-start.4 = (bf16[66,8,256]{2,1,0:T(8,128)(2,1)S(1)}, bf16[66,8,256]{2,1,0:T(8,128)(2,1)S(1)}, u32[]{:S(2)}, u32[]{:S(2)}) collective-permute-start(bf16[66,8,256]{2,1,0:T(8,128)(2,1)S(1)} %get-tuple-element.52), channel_id=1, source_target_pairs={{0,4},{4,0},{8,12},{12,8},{1,5},{5,1},{9,13},{13,9},{2,6},{6,2},{1... | collective-permute-start | bytes 811016 | tf_op jit(solution)/shard_map/ppermute | solution.py:29
  42.0 0.0 collective-permute-done.2.refs_1_.refs_11_
  42.1 2.5 %collective-permute-start.5 = (bf16[66,8,256]{2,1,0:T(8,128)(2,1)S(1)}, bf16[66,8,256]{2,1,0:T(8,128)(2,1)S(1)}, u32[]{:S(2)}, u32[]{:S(2)}) collective-permute-start(bf16[66,8,256]{2,1,0:T(8,128)(2,1)S(1)} %get-tuple-element.52), channel_id=1, source_target_pairs={{0,12},{4,8},{8,4},{12,0},{1,13},{5,9},{9,5},{13,1},{2,14},{6,10},... | collective-permute-start | bytes 811016 | tf_op jit(solution)/shard_map/ppermute | solution.py:29
  44.6 0.0 collective-permute-done.3.refs_3_.refs_13_
  44.6 2.8 %merge.1 = (bf16[1,2,512,1024]{3,2,1,0:T(8,128)(2,1)}, f32[4,128]{1,0:T(4,128)S(1)}) custom-call(bf16[66,8,640]{2,1,0:T(8,128)(2,1)S(1)} %cut.1.refs_0_, bf16[67,8,384]{2,1,0:T(8,128)(2,1)S(1)} %collective-permute-done.2.refs_1_.refs_11_, bf16[66,8,640]{2,1,0:T(8,128)(2,1)S(1)} %collective-permute-done.1.refs_2_.refs_3_, ...), custom_call_target="tpu_custom_call" | custom-call | flops 843448320 | bytes 3145728 | tf_op jit(solution)/shard_map/merge/pallas_call | solution.py:379
  47.4 0.4 ready.1.refs_0_
  47.9 0.9 %collective-permute-done.6.refs_2_ = bf16[66,8,384]{2,1,0:T(8,128)(2,1)S(1)} collective-permute-done((bf16[66,8,384]{2,1,0:T(8,128)(2,1)S(1)}, bf16[66,8,384]{2,1,0:T(8,128)(2,1)S(1)}, u32[]{:S(2)}, u32[]{:S(2)}) %collective-permute-start.6) | collective-permute-done | bytes 405536 | tf_op jit(solution)/shard_map/ppermute | solution.py:29
  48.8 1.0 %collective-permute-done.7.refs_5_ = bf16[66,8,384]{2,1,0:T(8,128)(2,1)S(1)} collective-permute-done((bf16[66,8,384]{2,1,0:T(8,128)(2,1)S(1)}, bf16[66,8,384]{2,1,0:T(8,128)(2,1)S(1)}, u32[]{:S(2)}, u32[]{:S(2)}) %collective-permute-start.7) | collective-permute-done | bytes 405536 | tf_op jit(solution)/shard_map/ppermute | solution.py:29
  49.9 2.8 %finish.2.refs_10_ = bf16[1,2,512,1024]{3,2,1,0:T(8,128)(2,1)} custom-call(bf16[66,8,640]{2,1,0:T(8,128)(2,1)S(1)} %cut.1.refs_0_, bf16[73,8,384]{2,1,0:T(8,128)(2,1)S(1)} %get-tuple-element.34.own.refs_1_, bf16[66,8,384]{2,1,0:T(8,128)(2,1)S(1)} %collective-permute-done.6.refs_2_, ...), custom_call_target="tpu_custom_call", output_to_operand_aliasing={{}: (13, {})} | custom-call | flops 843448320 | bytes 3145728 | tf_op jit(solution)/shard_map/finish/pallas_call | solution.py:418
  52.7 1.9 %collective-permute-done.4.refs_1_ = bf16[66,8,256]{2,1,0:T(8,128)(2,1)S(1)} collective-permute-done((bf16[66,8,256]{2,1,0:T(8,128)(2,1)S(1)}, bf16[66,8,256]{2,1,0:T(8,128)(2,1)S(1)}, u32[]{:S(2)}, u32[]{:S(2)}) %collective-permute-start.4) | collective-permute-done | bytes 270368 | tf_op jit(solution)/shard_map/ppermute | solution.py:29
  54.6 1.0 %collective-permute-done.5.refs_2_ = bf16[66,8,256]{2,1,0:T(8,128)(2,1)S(1)} collective-permute-done((bf16[66,8,256]{2,1,0:T(8,128)(2,1)S(1)}, bf16[66,8,256]{2,1,0:T(8,128)(2,1)S(1)}, u32[]{:S(2)}, u32[]{:S(2)}) %collective-permute-start.5) | collective-permute-done | bytes 270368 | tf_op jit(solution)/shard_map/ppermute | solution.py:29
  55.7 1.9 %finish.3 = bf16[1,2,512,1024]{3,2,1,0:T(8,128)(2,1)} custom-call(f32[2,264,512]{2,1,0:T(8,128)S(1)} %ready.1.refs_0_, bf16[66,8,256]{2,1,0:T(8,128)(2,1)S(1)} %collective-permute-done.4.refs_1_, bf16[66,8,256]{2,1,0:T(8,128)(2,1)S(1)} %collective-permute-done.5.refs_2_, ...), custom_call_target="tpu_custom_call", output_to_operand_aliasing={{}: (10, {})} | custom-call | flops 562298880 | bytes 2097152 | tf_op jit(solution)/shard_map/finish/pallas_call | solution.py:418
  (4 shorter events, 0.1 us)
Async XLA Ops:
  0.0 6.8 %copy-start.1 = (f32[2,2,1,1024]{3,2,1,0:T(1,128)S(1)}, f32[2,2,1,1024]{3,2,1,0:T(1,128)}, u32[]{:S(2)}) copy-start(f32[2,2,1,1024]{3,2,1,0:T(1,128)} %refs_5_.1) | copy-start | bytes 49156
  0.0 6.8 %copy-start.2 = (s32[2,2,1,512]{3,2,1,0:T(1,128)S(1)}, s32[2,2,1,512]{3,2,1,0:T(1,128)}, u32[]{:S(2)}) copy-start(s32[2,2,1,512]{3,2,1,0:T(1,128)} %refs_4_.1) | copy-start | bytes 24580
  0.0 6.8 %copy-start = (f32[2,2,1,8,512]{4,3,2,1,0:T(8,128)S(1)}, f32[2,2,1,8,512]{4,3,2,1,0:T(8,128)}, u32[]{:S(2)}) copy-start(f32[2,2,1,8,512]{4,3,2,1,0:T(8,128)} %refs_3_.1) | copy-start | bytes 196612
  1.3 29.8 %collective-permute-start.1 = (bf16[66,8,640]{2,1,0:T(8,128)(2,1)S(1)}, bf16[66,8,640]{2,1,0:T(8,128)(2,1)S(1)}, u32[]{:S(2)}, u32[]{:S(2)}) collective-permute-start(bf16[66,8,640]{2,1,0:T(8,128)(2,1)S(1)} %cut.1.refs_0_), channel_id=1, source_target_pairs={{0,8},{4,12},{8,0},{12,4},{1,9},{5,13},{9,1},{13,5},{2,10},{6,14},... | collective-permute-start | bytes 2027528 | tf_op jit(solution)/shard_map/ppermute | solution.py:29
  16.9 21.3 %collective-permute-start = (bf16[73,8,384]{2,1,0:T(8,128)(2,1)S(1)}, bf16[73,8,384]{2,1,0:T(8,128)(2,1)S(1)}, u32[]{:S(2)}, u32[]{:S(2)}) collective-permute-start(bf16[73,8,384]{2,1,0:T(8,128)(2,1)S(1)} %get-tuple-element.34.own.refs_1_), channel_id=1, source_target_pairs={{0,8},{4,12},{8,0},{12,4},{1,9},{5,13},{9,1},{13,5},{2,10},{6,14},... | collective-permute-start | bytes 1345544 | tf_op jit(solution)/shard_map/ppermute | solution.py:29
  22.1 20.0 %collective-permute-start.2 = (bf16[67,8,384]{2,1,0:T(8,128)(2,1)S(1)}, bf16[67,8,384]{2,1,0:T(8,128)(2,1)S(1)}, u32[]{:S(2)}, u32[]{:S(2)}) collective-permute-start(bf16[67,8,384]{2,1,0:T(8,128)(2,1)S(1)} %get-tuple-element.47), channel_id=1, source_target_pairs={{0,4},{4,0},{8,12},{12,8},{1,5},{5,1},{9,13},{13,9},{2,6},{6,2},{1... | collective-permute-start | bytes 1234952 | tf_op jit(solution)/shard_map/ppermute | solution.py:29
  24.0 20.6 %collective-permute-start.3 = (bf16[67,8,384]{2,1,0:T(8,128)(2,1)S(1)}, bf16[67,8,384]{2,1,0:T(8,128)(2,1)S(1)}, u32[]{:S(2)}, u32[]{:S(2)}) collective-permute-start(bf16[67,8,384]{2,1,0:T(8,128)(2,1)S(1)} %get-tuple-element.47), channel_id=1, source_target_pairs={{0,12},{4,8},{8,4},{12,0},{1,13},{5,9},{9,5},{13,1},{2,14},{6,10},... | collective-permute-start | bytes 1234952 | tf_op jit(solution)/shard_map/ppermute | solution.py:29
  31.1 17.7 %collective-permute-start.6 = (bf16[66,8,384]{2,1,0:T(8,128)(2,1)S(1)}, bf16[66,8,384]{2,1,0:T(8,128)(2,1)S(1)}, u32[]{:S(2)}, u32[]{:S(2)}) collective-permute-start(bf16[66,8,384]{2,1,0:T(8,128)(2,1)S(1)} %get-tuple-element.53), channel_id=1, source_target_pairs={{0,4},{4,0},{8,12},{12,8},{1,5},{5,1},{9,13},{13,9},{2,6},{6,2},{1... | collective-permute-start | bytes 1216520 | tf_op jit(solution)/shard_map/ppermute | solution.py:29
  34.2 15.6 %collective-permute-start.7 = (bf16[66,8,384]{2,1,0:T(8,128)(2,1)S(1)}, bf16[66,8,384]{2,1,0:T(8,128)(2,1)S(1)}, u32[]{:S(2)}, u32[]{:S(2)}) collective-permute-start(bf16[66,8,384]{2,1,0:T(8,128)(2,1)S(1)} %get-tuple-element.53), channel_id=1, source_target_pairs={{0,12},{4,8},{8,4},{12,0},{1,13},{5,9},{9,5},{13,1},{2,14},{6,10},... | collective-permute-start | bytes 1216520 | tf_op jit(solution)/shard_map/ppermute | solution.py:29
  40.1 14.5 %collective-permute-start.4 = (bf16[66,8,256]{2,1,0:T(8,128)(2,1)S(1)}, bf16[66,8,256]{2,1,0:T(8,128)(2,1)S(1)}, u32[]{:S(2)}, u32[]{:S(2)}) collective-permute-start(bf16[66,8,256]{2,1,0:T(8,128)(2,1)S(1)} %get-tuple-element.52), channel_id=1, source_target_pairs={{0,4},{4,0},{8,12},{12,8},{1,5},{5,1},{9,13},{13,9},{2,6},{6,2},{1... | collective-permute-start | bytes 811016 | tf_op jit(solution)/shard_map/ppermute | solution.py:29
  42.1 13.6 %collective-permute-start.5 = (bf16[66,8,256]{2,1,0:T(8,128)(2,1)S(1)}, bf16[66,8,256]{2,1,0:T(8,128)(2,1)S(1)}, u32[]{:S(2)}, u32[]{:S(2)}) collective-permute-start(bf16[66,8,256]{2,1,0:T(8,128)(2,1)S(1)} %get-tuple-element.52), channel_id=1, source_target_pairs={{0,12},{4,8},{8,4},{12,0},{1,13},{5,9},{9,5},{13,1},{2,14},{6,10},... | collective-permute-start | bytes 811016 | tf_op jit(solution)/shard_map/ppermute | solution.py:29

commit v6 on v5

--- a/solution.py
+++ b/solution.py
@@ -17,7 +17,6 @@
 TAPS = 8
 LANES = 128
 BLOCK = 384
-OUT_ROWS = 256
 FAR_PARTS = (640, 384)
 NEAR_PARTS = (384, 384, 256)
 DATA_TILES = 6
@@ -335,12 +334,10 @@
 
 def write_out(both, table, buffer, result, bins, sems):
     copies = []
-    for k, row in enumerate(range(0, buffer.shape[1], OUT_ROWS)):
-        rows = slice(row, row + OUT_ROWS)
-        merged = jnp.dot(table[rows, :], both, preferred_element_type=jnp.float32)
-        for half, part in enumerate(halves(merged)):
-            buffer[half, rows] = part.astype(jnp.bfloat16)
-        copies.append(pltpu.make_async_copy(buffer.at[:, rows], result.at[0, :, rows, bins], sems.at[k]))
+    for half, part in enumerate(halves(both)):
+        merged = jnp.dot(table[...], part, preferred_element_type=jnp.float32)
+        buffer[half] = merged.astype(jnp.bfloat16)
+        copies.append(pltpu.make_async_copy(buffer.at[half], result.at[0, half, :, bins], sems.at[half]))
         copies[-1].start()
     for copy in copies:
         copy.wait()
@@ -420,7 +417,7 @@
         out_shape=jax.ShapeDtypeStruct(prior.shape, prior.dtype),
         in_specs=[pl.BlockSpec(memory_space=pltpu.VMEM)] * len(operands) + [pl.BlockSpec(memory_space=pl.ANY)],
         out_specs=pl.BlockSpec(memory_space=pl.ANY),
-        scratch_shapes=[pltpu.VMEM((2, beams, width), prior.dtype), pltpu.SemaphoreType.DMA((beams // OUT_ROWS,))],
+        scratch_shapes=[pltpu.VMEM((2, beams, width), prior.dtype), pltpu.SemaphoreType.DMA((2,))],
         input_output_aliases={len(operands): 0},
         compiler_params=pltpu.CompilerParams(vmem_limit_bytes=16 * 2**20),
         cost_estimate=merge_cost(width, beams),

time: 57.9 us -> 57.8 us (level)
  no operation moved by 1% of the time
where the time goes in v6:
time: 57.8 us; the launch traced here: 57.4 us
  starting transfers between devices  26.2 us (45%)
  Pallas kernels  17.3 us (30%)
  blocking collectives  8.31 us (14%)
  waiting for transfers between devices  5.2 us (9%)
    ppermute x8, starting transfers between devices, partner(): return lax.ppermute(value, 'x', [(i, i ^ flip) for i in range(GROUP)])  26.2 us
    psum x1, blocking collectives, shards(): energy = lax.psum(energy, 'sec')  8.31 us
    pallas_call x3, Pallas kernels, make_table(): pl.pallas_call(table_kernel, out_shape=[jax.ShapeDtypeStruct(s, jnp.float...  6.6 us
    ppermute x8, waiting for transfers between devices, partner(): return lax.ppermute(value, 'x', [(i, i ^ flip) for i in range(GROUP)])  5.2 us
    pallas_call x2, Pallas kernels, finish(): pl.pallas_call(kernel, out_shape=jax.ShapeDtypeStruct(prior.shape, prior....  4.33 us
    pallas_call x1, Pallas kernels, merge_first(): pl.pallas_call(functools.partial(merge_kernel, cells), grid=(width // BLO...  2.84 us
    pallas_call x1, Pallas kernels, prepare(): pl.pallas_call(prepare_kernel, grid=(1,), out_shape=shapes, in_specs=[*se...  1.75 us
    pallas_call x1, Pallas kernels, cut(): pl.pallas_call(cut_kernel, out_shape=jax.ShapeDtypeStruct((2 * SPAN, TILE...  1.29 us
  transfers between devices with their start and end apart: 8, of which 4 were waited for; matrix products, arithmetic and copies ran while one was open for 0% of the time, Pallas kernels for 25%

profile of v6, /device:TPU:1, one launch (start us, length us, event | category | flops | bytes accessed | tf_op | source)
XLA Modules:
  0.0 57.4 jit_solution(16692885743174478265)
XLA Ops:
  0.0 0.0 copy-start.1
  0.0 0.0 copy-start.2
  0.0 1.3 %cut.1.refs_0_ = bf16[66,8,640]{2,1,0:T(8,128)(2,1)S(1)} custom-call(bf16[2,64,8,1024]{3,2,1,0:T(8,128)(2,1)} %bitcast.1), custom_call_target="tpu_custom_call" | custom-call | bytes 1600000 | tf_op jit(solution)/shard_map/cut/pallas_call | solution.py:85
  1.3 5.5 %collective-permute-start.1 = (bf16[66,8,640]{2,1,0:T(8,128)(2,1)S(1)}, bf16[66,8,640]{2,1,0:T(8,128)(2,1)S(1)}, u32[]{:S(2)}, u32[]{:S(2)}) collective-permute-start(bf16[66,8,640]{2,1,0:T(8,128)(2,1)S(1)} %cut.1.refs_0_), channel_id=1, source_target_pairs={{0,8},{4,12},{8,0},{12,4},{1,9},{5,13},{9,1},{13,5},{2,10},{6,14},... | collective-permute-start | bytes 2027528 | tf_op jit(solution)/shard_map/ppermute | solution.py:28
  6.8 0.0 copy-done.1
  6.8 0.0 copy-done.2
  6.8 0.0 copy-done
  6.8 1.7 %prepare.1 = (bf16[73,8,384]{2,1,0:T(8,128)(2,1)S(1)}, bf16[67,8,384]{2,1,0:T(8,128)(2,1)S(1)}, bf16[66,8,384]{2,1,0:T(8,128)(2,1)S(1)}, bf16[66,8,256]{2,1,0:T(...) custom-call(f32[2,2,1,8,512]{4,3,2,1,0:T(8,128)S(1)} %copy-done, ...), custom_call_target="tpu_custom_call" | custom-call | flops 1081344 | bytes 4000000 | tf_op jit(solution)/shard_map/prepare/pallas_call | solution.py:147
  8.6 8.3 %psum.7.energy.refs_10_ = f32[1,128]{1,0:T(1,128)S(1)} all-reduce(f32[1,128]{1,0:T(1,128)S(1)} %get-tuple-element.33), channel_id=1, replica_groups=mesh['rest'=32,'x'=4,'sec'=4] {'sec'}, use_global_device_ids=true, to_apply=%region_0.0 | all-reduce | flops 128 | bytes 1024 | tf_op jit(solution)/shard_map/psum | solution.py:437
  16.9 5.1 %collective-permute-start = (bf16[73,8,384]{2,1,0:T(8,128)(2,1)S(1)}, bf16[73,8,384]{2,1,0:T(8,128)(2,1)S(1)}, u32[]{:S(2)}, u32[]{:S(2)}) collective-permute-start(bf16[73,8,384]{2,1,0:T(8,128)(2,1)S(1)} %get-tuple-element.34.own.refs_1_), channel_id=1, source_target_pairs={{0,8},{4,12},{8,0},{12,4},{1,9},{5,13},{9,1},{13,5},{2,10},{6,14},... | collective-permute-start | bytes 1345544 | tf_op jit(solution)/shard_map/ppermute | solution.py:28
  22.1 1.9 %collective-permute-start.2 = (bf16[67,8,384]{2,1,0:T(8,128)(2,1)S(1)}, bf16[67,8,384]{2,1,0:T(8,128)(2,1)S(1)}, u32[]{:S(2)}, u32[]{:S(2)}) collective-permute-start(bf16[67,8,384]{2,1,0:T(8,128)(2,1)S(1)} %get-tuple-element.47), channel_id=1, source_target_pairs={{0,4},{4,0},{8,12},{12,8},{1,5},{5,1},{9,13},{13,9},{2,6},{6,2},{1... | collective-permute-start | bytes 1234952 | tf_op jit(solution)/shard_map/ppermute | solution.py:28
  24.0 2.2 %collective-permute-start.3 = (bf16[67,8,384]{2,1,0:T(8,128)(2,1)S(1)}, bf16[67,8,384]{2,1,0:T(8,128)(2,1)S(1)}, u32[]{:S(2)}, u32[]{:S(2)}) collective-permute-start(bf16[67,8,384]{2,1,0:T(8,128)(2,1)S(1)} %get-tuple-element.47), channel_id=1, source_target_pairs={{0,12},{4,8},{8,4},{12,0},{1,13},{5,9},{9,5},{13,1},{2,14},{6,10},... | collective-permute-start | bytes 1234952 | tf_op jit(solution)/shard_map/ppermute | solution.py:28
  26.2 2.9 %table.4 = (f32[512,528]{1,0:T(8,128)S(1)}, f32[4,1024]{1,0:T(4,128)S(1)}) custom-call(bf16[2,8,1024]{2,1,0:T(8,128)(2,1)S(1)} %get-tuple-element.38.data), custom_call_target="tpu_custom_call" | custom-call | flops 6144000 | bytes 2097152 | tf_op jit(solution)/shard_map/table/pallas_call | solution.py:242
  29.1 0.1 convert_element_type.10.refs_6_.refs_8_.refs_5_
  29.2 1.8 %table.3 = (f32[264,528]{1,0:T(8,128)S(1)}, f32[4,1024]{1,0:T(4,128)S(1)}) custom-call(bf16[2,8,1024]{2,1,0:T(8,128)(2,1)S(1)} %get-tuple-element.36.data), custom_call_target="tpu_custom_call" | custom-call | flops 3168000 | bytes 1081344 | tf_op jit(solution)/shard_map/table/pallas_call | solution.py:242
  31.1 0.0 collective-permute-done.1.refs_2_.refs_3_
  31.1 3.1 %collective-permute-start.6 = (bf16[66,8,384]{2,1,0:T(8,128)(2,1)S(1)}, bf16[66,8,384]{2,1,0:T(8,128)(2,1)S(1)}, u32[]{:S(2)}, u32[]{:S(2)}) collective-permute-start(bf16[66,8,384]{2,1,0:T(8,128)(2,1)S(1)} %get-tuple-element.53), channel_id=1, source_target_pairs={{0,4},{4,0},{8,12},{12,8},{1,5},{5,1},{9,13},{13,9},{2,6},{6,2},{1... | collective-permute-start | bytes 1216520 | tf_op jit(solution)/shard_map/ppermute | solution.py:28
  34.2 4.0 %collective-permute-start.7 = (bf16[66,8,384]{2,1,0:T(8,128)(2,1)S(1)}, bf16[66,8,384]{2,1,0:T(8,128)(2,1)S(1)}, u32[]{:S(2)}, u32[]{:S(2)}) collective-permute-start(bf16[66,8,384]{2,1,0:T(8,128)(2,1)S(1)} %get-tuple-element.53), channel_id=1, source_target_pairs={{0,12},{4,8},{8,4},{12,0},{1,13},{5,9},{9,5},{13,1},{2,14},{6,10},... | collective-permute-start | bytes 1216520 | tf_op jit(solution)/shard_map/ppermute | solution.py:28
  38.2 0.0 collective-permute-done.data.refs_12_.two.refs_4_
  38.2 1.9 %table.5 = (f32[264,528]{1,0:T(8,128)S(1)}, f32[4,1024]{1,0:T(4,128)S(1)}) custom-call(bf16[73,8,384]{2,1,0:T(8,128)(2,1)S(1)} %collective-permute-done.data.refs_12_.two.refs_4_), custom_call_target="tpu_custom_call" | custom-call | flops 3168000 | bytes 1081344 | tf_op jit(solution)/shard_map/table/pallas_call | solution.py:242
  40.1 1.9 %collective-permute-start.4 = (bf16[66,8,256]{2,1,0:T(8,128)(2,1)S(1)}, bf16[66,8,256]{2,1,0:T(8,128)(2,1)S(1)}, u32[]{:S(2)}, u32[]{:S(2)}) collective-permute-start(bf16[66,8,256]{2,1,0:T(8,128)(2,1)S(1)} %get-tuple-element.52), channel_id=1, source_target_pairs={{0,4},{4,0},{8,12},{12,8},{1,5},{5,1},{9,13},{13,9},{2,6},{6,2},{1... | collective-permute-start | bytes 811016 | tf_op jit(solution)/shard_map/ppermute | solution.py:28
  42.0 0.0 collective-permute-done.2.refs_1_.refs_11_
  42.1 2.5 %collective-permute-start.5 = (bf16[66,8,256]{2,1,0:T(8,128)(2,1)S(1)}, bf16[66,8,256]{2,1,0:T(8,128)(2,1)S(1)}, u32[]{:S(2)}, u32[]{:S(2)}) collective-permute-start(bf16[66,8,256]{2,1,0:T(8,128)(2,1)S(1)} %get-tuple-element.52), channel_id=1, source_target_pairs={{0,12},{4,8},{8,4},{12,0},{1,13},{5,9},{9,5},{13,1},{2,14},{6,10},... | collective-permute-start | bytes 811016 | tf_op jit(solution)/shard_map/ppermute | solution.py:28
  44.6 0.0 collective-permute-done.3.refs_3_.refs_13_
  44.6 2.8 %merge.1 = (bf16[1,2,512,1024]{3,2,1,0:T(8,128)(2,1)}, f32[4,128]{1,0:T(4,128)S(1)}) custom-call(bf16[66,8,640]{2,1,0:T(8,128)(2,1)S(1)} %cut.1.refs_0_, bf16[67,8,384]{2,1,0:T(8,128)(2,1)S(1)} %collective-permute-done.2.refs_1_.refs_11_, bf16[66,8,640]{2,1,0:T(8,128)(2,1)S(1)} %collective-permute-done.1.refs_2_.refs_3_, ...), custom_call_target="tpu_custom_call" | custom-call | flops 843448320 | bytes 3145728 | tf_op jit(solution)/shard_map/merge/pallas_call | solution.py:376
  47.4 0.4 ready.1.refs_0_
  47.9 0.9 %collective-permute-done.6.refs_2_ = bf16[66,8,384]{2,1,0:T(8,128)(2,1)S(1)} collective-permute-done((bf16[66,8,384]{2,1,0:T(8,128)(2,1)S(1)}, bf16[66,8,384]{2,1,0:T(8,128)(2,1)S(1)}, u32[]{:S(2)}, u32[]{:S(2)}) %collective-permute-start.6) | collective-permute-done | bytes 405536 | tf_op jit(solution)/shard_map/ppermute | solution.py:28
  48.8 1.0 %collective-permute-done.7.refs_5_ = bf16[66,8,384]{2,1,0:T(8,128)(2,1)S(1)} collective-permute-done((bf16[66,8,384]{2,1,0:T(8,128)(2,1)S(1)}, bf16[66,8,384]{2,1,0:T(8,128)(2,1)S(1)}, u32[]{:S(2)}, u32[]{:S(2)}) %collective-permute-start.7) | collective-permute-done | bytes 405536 | tf_op jit(solution)/shard_map/ppermute | solution.py:28
  49.9 2.6 %finish.2.refs_10_ = bf16[1,2,512,1024]{3,2,1,0:T(8,128)(2,1)} custom-call(bf16[66,8,640]{2,1,0:T(8,128)(2,1)S(1)} %cut.1.refs_0_, bf16[73,8,384]{2,1,0:T(8,128)(2,1)S(1)} %get-tuple-element.34.own.refs_1_, bf16[66,8,384]{2,1,0:T(8,128)(2,1)S(1)} %collective-permute-done.6.refs_2_, ...), custom_call_target="tpu_custom_call", output_to_operand_aliasing={{}: (13, {})} | custom-call | flops 843448320 | bytes 3145728 | tf_op jit(solution)/shard_map/finish/pallas_call | solution.py:415
  52.5 2.2 %collective-permute-done.4.refs_1_ = bf16[66,8,256]{2,1,0:T(8,128)(2,1)S(1)} collective-permute-done((bf16[66,8,256]{2,1,0:T(8,128)(2,1)S(1)}, bf16[66,8,256]{2,1,0:T(8,128)(2,1)S(1)}, u32[]{:S(2)}, u32[]{:S(2)}) %collective-permute-start.4) | collective-permute-done | bytes 270368 | tf_op jit(solution)/shard_map/ppermute | solution.py:28
  54.6 1.0 %collective-permute-done.5.refs_2_ = bf16[66,8,256]{2,1,0:T(8,128)(2,1)S(1)} collective-permute-done((bf16[66,8,256]{2,1,0:T(8,128)(2,1)S(1)}, bf16[66,8,256]{2,1,0:T(8,128)(2,1)S(1)}, u32[]{:S(2)}, u32[]{:S(2)}) %collective-permute-start.5) | collective-permute-done | bytes 270368 | tf_op jit(solution)/shard_map/ppermute | solution.py:28
  55.7 1.8 %finish.3 = bf16[1,2,512,1024]{3,2,1,0:T(8,128)(2,1)} custom-call(f32[2,264,512]{2,1,0:T(8,128)S(1)} %ready.1.refs_0_, bf16[66,8,256]{2,1,0:T(8,128)(2,1)S(1)} %collective-permute-done.4.refs_1_, bf16[66,8,256]{2,1,0:T(8,128)(2,1)S(1)} %collective-permute-done.5.refs_2_, ...), custom_call_target="tpu_custom_call", output_to_operand_aliasing={{}: (10, {})} | custom-call | flops 562298880 | bytes 2097152 | tf_op jit(solution)/shard_map/finish/pallas_call | solution.py:415
  (4 shorter events, 0.1 us)
Async XLA Ops:
  0.0 6.8 %copy-start.1 = (f32[2,2,1,1024]{3,2,1,0:T(1,128)S(1)}, f32[2,2,1,1024]{3,2,1,0:T(1,128)}, u32[]{:S(2)}) copy-start(f32[2,2,1,1024]{3,2,1,0:T(1,128)} %refs_5_.1) | copy-start | bytes 49156
  0.0 6.8 %copy-start.2 = (s32[2,2,1,512]{3,2,1,0:T(1,128)S(1)}, s32[2,2,1,512]{3,2,1,0:T(1,128)}, u32[]{:S(2)}) copy-start(s32[2,2,1,512]{3,2,1,0:T(1,128)} %refs_4_.1) | copy-start | bytes 24580
  0.0 6.8 %copy-start = (f32[2,2,1,8,512]{4,3,2,1,0:T(8,128)S(1)}, f32[2,2,1,8,512]{4,3,2,1,0:T(8,128)}, u32[]{:S(2)}) copy-start(f32[2,2,1,8,512]{4,3,2,1,0:T(8,128)} %refs_3_.1) | copy-start | bytes 196612
  1.3 29.8 %collective-permute-start.1 = (bf16[66,8,640]{2,1,0:T(8,128)(2,1)S(1)}, bf16[66,8,640]{2,1,0:T(8,128)(2,1)S(1)}, u32[]{:S(2)}, u32[]{:S(2)}) collective-permute-start(bf16[66,8,640]{2,1,0:T(8,128)(2,1)S(1)} %cut.1.refs_0_), channel_id=1, source_target_pairs={{0,8},{4,12},{8,0},{12,4},{1,9},{5,13},{9,1},{13,5},{2,10},{6,14},... | collective-permute-start | bytes 2027528 | tf_op jit(solution)/shard_map/ppermute | solution.py:28
  16.9 21.3 %collective-permute-start = (bf16[73,8,384]{2,1,0:T(8,128)(2,1)S(1)}, bf16[73,8,384]{2,1,0:T(8,128)(2,1)S(1)}, u32[]{:S(2)}, u32[]{:S(2)}) collective-permute-start(bf16[73,8,384]{2,1,0:T(8,128)(2,1)S(1)} %get-tuple-element.34.own.refs_1_), channel_id=1, source_target_pairs={{0,8},{4,12},{8,0},{12,4},{1,9},{5,13},{9,1},{13,5},{2,10},{6,14},... | collective-permute-start | bytes 1345544 | tf_op jit(solution)/shard_map/ppermute | solution.py:28
  22.1 20.0 %collective-permute-start.2 = (bf16[67,8,384]{2,1,0:T(8,128)(2,1)S(1)}, bf16[67,8,384]{2,1,0:T(8,128)(2,1)S(1)}, u32[]{:S(2)}, u32[]{:S(2)}) collective-permute-start(bf16[67,8,384]{2,1,0:T(8,128)(2,1)S(1)} %get-tuple-element.47), channel_id=1, source_target_pairs={{0,4},{4,0},{8,12},{12,8},{1,5},{5,1},{9,13},{13,9},{2,6},{6,2},{1... | collective-permute-start | bytes 1234952 | tf_op jit(solution)/shard_map/ppermute | solution.py:28
  24.0 20.6 %collective-permute-start.3 = (bf16[67,8,384]{2,1,0:T(8,128)(2,1)S(1)}, bf16[67,8,384]{2,1,0:T(8,128)(2,1)S(1)}, u32[]{:S(2)}, u32[]{:S(2)}) collective-permute-start(bf16[67,8,384]{2,1,0:T(8,128)(2,1)S(1)} %get-tuple-element.47), channel_id=1, source_target_pairs={{0,12},{4,8},{8,4},{12,0},{1,13},{5,9},{9,5},{13,1},{2,14},{6,10},... | collective-permute-start | bytes 1234952 | tf_op jit(solution)/shard_map/ppermute | solution.py:28
  31.1 17.7 %collective-permute-start.6 = (bf16[66,8,384]{2,1,0:T(8,128)(2,1)S(1)}, bf16[66,8,384]{2,1,0:T(8,128)(2,1)S(1)}, u32[]{:S(2)}, u32[]{:S(2)}) collective-permute-start(bf16[66,8,384]{2,1,0:T(8,128)(2,1)S(1)} %get-tuple-element.53), channel_id=1, source_target_pairs={{0,4},{4,0},{8,12},{12,8},{1,5},{5,1},{9,13},{13,9},{2,6},{6,2},{1... | collective-permute-start | bytes 1216520 | tf_op jit(solution)/shard_map/ppermute | solution.py:28
  34.2 15.6 %collective-permute-start.7 = (bf16[66,8,384]{2,1,0:T(8,128)(2,1)S(1)}, bf16[66,8,384]{2,1,0:T(8,128)(2,1)S(1)}, u32[]{:S(2)}, u32[]{:S(2)}) collective-permute-start(bf16[66,8,384]{2,1,0:T(8,128)(2,1)S(1)} %get-tuple-element.53), channel_id=1, source_target_pairs={{0,12},{4,8},{8,4},{12,0},{1,13},{5,9},{9,5},{13,1},{2,14},{6,10},... | collective-permute-start | bytes 1216520 | tf_op jit(solution)/shard_map/ppermute | solution.py:28
  40.1 14.5 %collective-permute-start.4 = (bf16[66,8,256]{2,1,0:T(8,128)(2,1)S(1)}, bf16[66,8,256]{2,1,0:T(8,128)(2,1)S(1)}, u32[]{:S(2)}, u32[]{:S(2)}) collective-permute-start(bf16[66,8,256]{2,1,0:T(8,128)(2,1)S(1)} %get-tuple-element.52), channel_id=1, source_target_pairs={{0,4},{4,0},{8,12},{12,8},{1,5},{5,1},{9,13},{13,9},{2,6},{6,2},{1... | collective-permute-start | bytes 811016 | tf_op jit(solution)/shard_map/ppermute | solution.py:28
  42.1 13.6 %collective-permute-start.5 = (bf16[66,8,256]{2,1,0:T(8,128)(2,1)S(1)}, bf16[66,8,256]{2,1,0:T(8,128)(2,1)S(1)}, u32[]{:S(2)}, u32[]{:S(2)}) collective-permute-start(bf16[66,8,256]{2,1,0:T(8,128)(2,1)S(1)} %get-tuple-element.52), channel_id=1, source_target_pairs={{0,12},{4,8},{8,4},{12,0},{1,13},{5,9},{9,5},{13,1},{2,14},{6,10},... | collective-permute-start | bytes 811016 | tf_op jit(solution)/shard_map/ppermute | solution.py:28
